TPU v7x, 256 devices: a whole 4x4x8 slice. The times are simulated.
256 devices in a mesh: owner: 64 (over x, z, core), dense: 4 (over y).
Axes of the slice: x: 4, y: 4, z: 8, core: 2. Of those that a mesh axis runs over, the one named last changes fastest.
Arguments:
- owners: int32 [65536, 13, 4], P(('owner', 'dense')), may hold values from 0 to 63, all different within a row; in each aligned block of 3328 rows (0 to 3327, 3328 to 6655, ..., all dimensions but the last counted through in order) at most 416 rows name the same one
- local_rows: int32 [65536, 13, 4], P(('owner', 'dense')), may hold values from 0 to 2047, as said below
- weights: float32 [65536, 13, 4], P(('owner', 'dense')), may hold values from 0.25 to 4
- labels: bfloat16 [65536], P(('owner', 'dense')), may hold values from 0 to 1
- table: float32 [131072, 128], P('owner'), may hold values from -6 to 6
- accum: float32 [131072], P('owner'), may hold values from 0.0001 to 0.01
- w_in: bfloat16 [1664, 4096], P(None, 'dense'), may hold values from -0.15625 to 0.15625
- b_in: bfloat16 [4096], P('dense'), may hold values from -3 to 3
- w_out: bfloat16 [4096], P('dense'), may hold values from -0.29882812 to 0.29882812
Outputs:
- new_table: float32 [131072, 128], P('owner')
- new_accum: float32 [131072], P('owner')
- weight_grad: float32 [65536, 13, 4], P(('owner', 'dense'))
Inputs may be any that keep to these rules, and one draw needn't show every extreme that they name: The 4 owners of one bag differ. Among the bags of one device (3328 of them, aligned blocks of rows), at most 416 name one owner. Among the ids of one device's samples (13312 of them, aligned blocks of rows), exactly 104 distinct values of local_rows occur.
All inputs are finite; a program needn't handle non-finite values.
Results may differ from a plain program's by a relative error of at most 0.0056.
Values may be sent and summed in bfloat16 or wider, within the bound.
No kernel may reach another device: no remote copies, remote signals or barrier semaphores. Data moves between devices by JAX's collectives and lax.ppermute only.
A program may use at most 128 MiB of HBM per device.

v0:
```python
import jax
import jax.numpy as jnp
from jax import lax
from jax.sharding import PartitionSpec as P

step_size = 0.5


def silu_slope(preact, sigma_pre):
    return sigma_pre * (1.0 + preact * (1.0 - sigma_pre))


def local(owners, local_rows, weights, labels, table, accum, w_in, b_in, w_out):
    samples, fields, bag_len = owners.shape
    emb_width = table.shape[1]
    table_rows = table.shape[0]
    groups = lax.axis_size("owner")
    slot_total = samples * fields * bag_len
    capacity = 2 * slot_total // groups
    own_flat = owners.reshape(slot_total)
    local_flat = local_rows.reshape(slot_total)
    owner_marks = (own_flat[None, :] == jnp.arange(groups, dtype=jnp.int32)[:, None]).astype(
        jnp.int32
    )
    earlier = jnp.cumsum(owner_marks, axis=1) - owner_marks
    slot_rank = jnp.sum(earlier * owner_marks, axis=0)
    slot_place = own_flat * capacity + slot_rank
    send_rows = jnp.zeros((groups * capacity,), jnp.int32).at[slot_place].set(local_flat)
    send_rows = send_rows.reshape(groups, capacity)
    asked_piece = lax.all_to_all(send_rows, "owner", split_axis=0, concat_axis=0, tiled=True)
    found_rows = table[asked_piece].astype(jnp.bfloat16)
    returned = lax.all_to_all(found_rows, "owner", split_axis=0, concat_axis=0, tiled=True)
    looked = returned.reshape(groups * capacity, emb_width)[slot_place]
    looked = looked.reshape(samples, fields, bag_len, emb_width)
    looked_f = looked.astype(jnp.float32)
    weight_sums = jnp.sum(weights, axis=-1)
    pooled = jnp.sum(weights[..., None] * looked_f, axis=2) / weight_sums[..., None]
    inputs = pooled.astype(jnp.bfloat16).reshape(samples, fields * emb_width)
    all_inputs, all_labels = (
        lax.all_gather(inputs, "dense", axis=0, tiled=True),
        lax.all_gather(labels, "dense", axis=0, tiled=True),
    )
    out_proj = w_out.astype(jnp.float32)
    preact = jnp.dot(all_inputs, w_in, preferred_element_type=jnp.float32) + b_in.astype(
        jnp.float32
    )
    sigma_pre = jax.nn.sigmoid(preact)
    partial_logits = jnp.sum(preact * sigma_pre * out_proj, axis=-1)
    logits = lax.psum(partial_logits, "dense")
    logit_grad = jax.nn.sigmoid(logits) - all_labels.astype(jnp.float32)
    dhidden = (logit_grad[:, None] * out_proj * silu_slope(preact, sigma_pre)).astype(jnp.bfloat16)
    dinputs = lax.psum_scatter(
        lax.dot_general(
            dhidden, w_in, (((1,), (1,)), ((), ())), preferred_element_type=jnp.float32
        ),
        "dense",
        scatter_dimension=0,
        tiled=True,
    )
    dpooled = dinputs.reshape(samples, fields, emb_width)
    along = jnp.sum(looked_f * dpooled[:, :, None, :], axis=-1)
    centre = jnp.sum(pooled * dpooled, axis=-1)
    weight_grad = (along - centre[..., None]) / weight_sums[..., None]
    slot_grad = ((weights / weight_sums[..., None])[..., None] * dpooled[:, :, None, :]).astype(
        jnp.bfloat16
    )
    slot_rows = slot_grad.reshape(slot_total, emb_width)
    send_grads = (
        jnp.zeros((groups * capacity, emb_width), jnp.bfloat16).at[slot_place].set(slot_rows)
    )
    send_grads = send_grads.reshape(groups, capacity, emb_width)
    got_grads = lax.all_to_all(send_grads, "owner", split_axis=0, concat_axis=0, tiled=True)
    row_part = (
        jnp.zeros((table_rows, emb_width), jnp.float32)
        .at[asked_piece.reshape(-1)]
        .add(got_grads.reshape(-1, emb_width).astype(jnp.float32))
    )
    row_grad = lax.psum(row_part.astype(jnp.bfloat16), "dense").astype(jnp.float32)
    new_accum = accum + jnp.mean(row_grad * row_grad, axis=-1)
    new_table = table - step_size * row_grad / jnp.sqrt(new_accum)[:, None]
    return (new_table, new_accum, weight_grad)


def solution(mesh):
    placed = (
        P(("owner", "dense"), None, None),
        P(("owner", "dense"), None, None),
        P(("owner", "dense"), None, None),
        P(("owner", "dense")),
        P("owner", None),
        P("owner"),
        P(None, "dense"),
        P("dense"),
        P("dense"),
    )
    return jax.shard_map(
        local,
        mesh=mesh,
        in_specs=placed,
        out_specs=(P("owner", None), P("owner"), P(("owner", "dense"), None, None)),
        check_vma=False,
    )
```

profile of v0, /device:TPU:1, one launch (start us, length us, event | category | flops | bytes accessed | tf_op | source)
XLA Modules:
  0.0 1073.5 jit_solution(17878568146684129480)
XLA Ops:
  8.2 3.3 copy.32
  16.1 3.2 copy.33
  19.3 2.8 reshape.200
  26.1 38.2 %reduce-window.6 = s32[64,104,128]{2,1,0:T(8,128)} reduce-window(s32[64,104,128]{2,1,0:T(8,128)} %fusion.7, s32[]{:T(128)} %constant.10.clone.1), window={size=1x1x128 pad=0_0x0_0x127_0}, to_apply=%region_0.0 | reduce-window | flops 108199936 | bytes 6815748 | tf_op jit(solution)/shard_map/reduce-window
  64.3 4.6 slice_reduce_fusion
  69.9 3.3 select_reduce_fusion
  73.9 50.0 %scatter_custom_fusion = s32[26624]{0:T(1024)} fusion(s32[13312]{0:T(1024)S(1)} %bitcast.30, s32[13312]{0:T(1024)} %reshape.200, s32[]{:T(128)} %constant.10.clone.1), kind=kCustom, calls=%fused_computation.43 | custom fusion | bytes 107008 | tf_op jit(solution)/shard_map/scatter | solution.py:28
  125.0 23.1 %all_to_all.22 = s32[64,1,416]{2,1,0:T(1,128)S(1)} all-to-all(s32[64,1,416]{2,1,0:T(1,128)S(1)} %all_to_all.14), channel_id=1, replica_groups=mesh['owner'=64,'dense'=4] {'owner'}, dimensions={0} | all-to-all | bytes 212992 | tf_op jit(solution)/shard_map/all_to_all | solution.py:30
  150.9 90.2 %gather_fusion = bf16[26624,128]{1,0:T(8,128)(2,1)} fusion(f32[2048,128]{1,0:T(8,128)} %param.13, s32[26624]{0:T(1024)S(1)} %broadcast_clamp_fusion), kind=kCustom, calls=%fused_computation | custom fusion | bytes 13737984 | tf_op jit(solution)/shard_map/gather | solution.py:31
  241.1 5.6 all-to-all-start.1
  251.2 147.6 %all-to-all-done.1 = bf16[64,416,128]{2,1,0:T(8,128)(2,1)} async-done(((bf16[64,416,128]{2,1,0:T(8,128)(2,1)}), bf16[64,416,128]{2,1,0:T(8,128)(2,1)}, u32[]{:S(2)}, u32[]{:S(2)}) %all-to-all-start.1) | async-done | bytes 6815776 | tf_op jit(solution)/shard_map/all_to_all | solution.py:32
  398.8 52.8 %gather_fusion.1 = bf16[13312,128]{1,0:T(8,128)(2,1)} fusion(bf16[26624,128]{1,0:T(8,128)(2,1)} %bitcast.5, s32[13312]{0:T(1024)} %broadcast_clamp_fusion.1), kind=kCustom, calls=%fused_computation.1 | custom fusion | bytes 6868992 | tf_op jit(solution)/shard_map/gather | solution.py:33
  451.6 6.6 fusion.2
  463.7 8.0 all-gather
  472.4 35.2 %all-gather.3.cloned.1.call-done = bf16[1024,1664]{0,1:T(8,128)(2,1)} async-done(((bf16[256,1664]{0,1:T(8,128)(2,1)}), bf16[1024,1664]{0,1:T(8,128)(2,1)}) %all-gather.3.cloned.1.call-update) | async-done | bytes 3407888 | tf_op jit(solution)/shard_map/all_gather | solution.py:40
  507.6 9.0 multiply_reduce_fusion
  516.6 7.9 psum.14
  524.5 10.3 fusion.8
  534.8 73.0 %reduce-scatter.2.cloned.1.call-done = f32[256,1664]{1,0:T(8,128)} async-done(((f32[1024,1664]{1,0:T(8,128)}), f32[256,1664]{1,0:T(8,128)}) %reduce-scatter.2.cloned.1.call-update) | async-done | bytes 1703952 | tf_op jit(solution)/shard_map/reduce_scatter | solution.py:52
  607.9 2.9 copy.39
  610.8 3.0 copy.40
  613.8 3.5 multiply_reduce_fusion.1
  617.3 7.6 fusion.3
  624.9 4.2 subtract_divide_fusion
  631.2 5.6 mul.117
  636.9 44.7 %scatter_custom_fusion.1 = bf16[26624,128]{1,0:T(8,128)(2,1)} fusion(s32[13312]{0:T(1024)} %bitcast.32, f32[13312,128]{1,0:T(8,128)} %bitcast.24, f32[13312]{0:T(1024)S(1)} %mul.104, bf16[]{:T(256)} %constant.14.clone.1), kind=kCustom, calls=%fused_computation.15 | custom fusion | flops 3407872 | bytes 13685248 | tf_op jit(solution)/shard_map/scatter | solution.py:69
  681.6 10.9 %all-to-all-start.2 = ((bf16[64,416,128]{2,1,0:T(8,128)(2,1)}), bf16[64,416,128]{2,1,0:T(8,128)(2,1)}, u32[]{:S(2)}, u32[]{:S(2)}) async-start(bf16[64,416,128]{2,1,0:T(8,128)(2,1)} %bitcast.25), calls=%async_computation.3 | async-start | bytes 13631488 | tf_op jit(solution)/shard_map/all_to_all | solution.py:72
  695.4 149.2 %all-to-all-done.2 = bf16[64,416,128]{2,1,0:T(8,128)(2,1)} async-done(((bf16[64,416,128]{2,1,0:T(8,128)(2,1)}), bf16[64,416,128]{2,1,0:T(8,128)(2,1)}, u32[]{:S(2)}, u32[]{:S(2)}) %all-to-all-start.2) | async-done | bytes 6815776 | tf_op jit(solution)/shard_map/all_to_all | solution.py:72
  844.6 145.4 %scatter_custom_fusion.2 = f32[2048,128]{1,0:T(8,128)} fusion(s32[26624]{0:T(1024)} %bitcast.34, bf16[26624,128]{1,0:T(8,128)(2,1)} %bitcast.14, f32[]{:T(128)} %constant.9.clone.1), kind=kCustom, calls=%fused_computation.5 | custom fusion | flops 6815744 | bytes 7864832 | tf_op jit(solution)/shard_map/scatter-add | solution.py:76
  992.1 3.0 copy.42
  995.1 67.0 %all-reduce.2.cloned.1.call-done = bf16[2048,128]{1,0:T(8,128)(2,1)} async-done(((bf16[2048,128]{1,0:T(8,128)(2,1)}), bf16[2048,128]{1,0:T(8,128)(2,1)}) %all-reduce.2.cloned.1.call-update) | async-done | bytes 524304 | tf_op jit(solution)/shard_map/psum | solution.py:78
  1064.1 2.7 fusion.14
  (53 shorter events, 35.0 us)
Async XLA Ops:
  7.2 500.5 %copy-start = (bf16[1664,1024]{1,0:T(8,128)(2,1)S(1)}, bf16[1664,1024]{1,0:T(8,128)(2,1)}, u32[]{:S(2)}) copy-start(bf16[1664,1024]{1,0:T(8,128)(2,1)} %param.15) | copy-start | bytes 10223620
  73.3 0.6 copy-start.4
  148.1 0.6 copy-start.2
  241.1 6.1 copy-start.5
  241.1 157.7 %all-to-all-start.1 = ((bf16[64,416,128]{2,1,0:T(8,128)(2,1)}), bf16[64,416,128]{2,1,0:T(8,128)(2,1)}, u32[]{:S(2)}, u32[]{:S(2)}) async-start(bf16[64,416,128]{2,1,0:T(8,128)(2,1)} %bitcast.26), calls=%async_computation.1 | async-start | bytes 13631488 | tf_op jit(solution)/shard_map/all_to_all | solution.py:32
  246.7 261.0 %all-gather.3.cloned.1.call-start = ((), (), s32[]{:S(2)}) async-start(), calls=%async_computation.4 | async-start | bytes 4259840 | tf_op jit(solution)/shard_map/all_gather | solution.py:40
  458.3 1.3 copy-start.1
  459.6 4.1 copy-start.8
  459.6 12.1 %copy-start.7 = (bf16[1024]{0:T(1024)(128)(2,1)S(1)}, bf16[1024]{0:T(1024)(128)(2,1)}, u32[]{:S(2)}) copy-start(bf16[1024]{0:T(1024)(128)(2,1)} %param.16) | copy-start | bytes 6148
  463.7 144.2 %reduce-scatter.2.cloned.1.call-start = ((), (), s32[]{:S(2)}) async-start(), calls=%async_computation.5 | async-start | bytes 8519680 | tf_op jit(solution)/shard_map/reduce_scatter | solution.py:52
  681.5 11.0 %copy-start.3 = (s32[64,1,416]{2,1,0:T(1,128)S(1)}, s32[64,1,416]{2,1,0:T(1,128)}, u32[]{:S(2)}) copy-start(s32[64,1,416]{2,1,0:T(1,128)} %copy-done.2) | copy-start | bytes 319492
  681.6 163.0 %all-to-all-start.2 = ((bf16[64,416,128]{2,1,0:T(8,128)(2,1)}), bf16[64,416,128]{2,1,0:T(8,128)(2,1)}, u32[]{:S(2)}, u32[]{:S(2)}) async-start(bf16[64,416,128]{2,1,0:T(8,128)(2,1)} %bitcast.25), calls=%async_computation.3 | async-start | bytes 13631488 | tf_op jit(solution)/shard_map/all_to_all | solution.py:72
  692.5 369.6 %all-reduce.2.cloned.1.call-start = ((), (), s32[]{:S(2)}) async-start(), calls=%async_computation.6 | async-start | bytes 1048576 | tf_op jit(solution)/shard_map/psum | solution.py:78
  990.0 73.5 %copy-start.6 = (f32[2048]{0:T(1024)S(1)}, f32[2048]{0:T(1024)}, u32[]{:S(2)}) copy-start(f32[2048]{0:T(1024)} %param.14) | copy-start | bytes 24580
Sparse Core Ops, SparseCore 0:
  463.8 43.7 all-gather.2
  535.0 72.8 reduce-scatter.1
  992.2 69.8 all-reduce.1
where the time goes:
time: 1090 us; the launch traced here: 1070 us
  waiting for transfers between devices  472 us (43%)
  other arithmetic  271 us (25%)
  local copies, waits for them, and re-layouts  241 us (22%)
  blocking collectives  39 us (4%)
  matrix products  19.3 us (2%)
  starting transfers between devices  17.1 us (2%)
  between operations  14.2 us (1%)
    all_to_all x1, waiting for transfers between devices, local(): lax.all_to_all(send_grads, 'owner', split_axis=0, concat_axis=0, tiled=True)  149 us
    all_to_all x1, waiting for transfers between devices, local(): lax.all_to_all(found_rows, 'owner', split_axis=0, concat_axis=0, tiled=True)  148 us
    scatter-add x1, other arithmetic, local(): row_part = jnp.zeros((table_rows, emb_width), jnp.float32).at[asked_piece...  145 us
    gather x1, local copies, waits for them, and re-layouts, local(): found_rows = table[asked_piece].astype(jnp.bfloat16)  90.2 us
    reduce_scatter x1, waiting for transfers between devices, local(): lax.psum_scatter(lax.dot_general(dhidden, w_in, (((1,), (1,)), ((), ())),...  73 us
    psum x1, waiting for transfers between devices, local(): lax.psum(row_part.astype(jnp.bfloat16), 'dense').astype(jnp.float32)  67 us
    gather x1, local copies, waits for them, and re-layouts, local(): looked = returned.reshape(groups * capacity, emb_width)[slot_place]  52.8 us
    scatter x1, local copies, waits for them, and re-layouts, local(): jnp.zeros((groups * capacity,), jnp.int32).at[slot_place].set(local_flat)  50 us
  transfers between devices with their start and end apart: 5, of which 5 were waited for; matrix products, arithmetic and copies ran while one was open for 1% of the time, Pallas kernels for 0%

commit v1 on v0

v1 whole, which is shorter than its diff:
```python
import functools

import jax
import jax.numpy as jnp
from jax import lax
from jax.experimental import pallas as pl
from jax.experimental.pallas import tpu as pltpu
from jax.sharding import PartitionSpec as P

step_size = 0.5
UNIQ = 104
ROWS_DEV = 2048
LANES = 128
VMEM_LIMIT = 56 * 1024 * 1024
f32, bf16, i32 = jnp.float32, jnp.bfloat16, jnp.int32


def dot(a, b, dims=((1,), (0,))):
    return lax.dot_general(a, b, (dims, ((), ())), preferred_element_type=f32)


def params(sem=None):
    return pltpu.CompilerParams(vmem_limit_bytes=VMEM_LIMIT, dimension_semantics=sem)


def index_kernel(own_ref, loc_ref, w_ref, list_ref, u_ref, c_ref):
    fields, bag_len, samples = own_ref.shape
    groups = u_ref.shape[0]
    his = ROWS_DEV // LANES
    lo_iota = lax.broadcasted_iota(i32, (LANES, samples), 0)
    hi_iota = lax.broadcasted_iota(i32, (his, samples), 0)

    def marks(row):
        lo = jnp.where(lo_iota == (row & (LANES - 1)), 1.0, 0.0).astype(bf16)
        hi = jnp.where(hi_iota == (row >> 7), 1.0, 0.0)
        return lo, hi

    count = jnp.zeros((his, LANES), f32)
    for f in range(fields):
        for j in range(bag_len):
            lo, hi = marks(loc_ref[f, j : j + 1, :])
            count = count + dot(hi.astype(bf16), lo, ((1,), (1,)))
    present = jnp.where(count > 0.5, 1.0, 0.0)
    tri = jnp.where(
        lax.broadcasted_iota(i32, (LANES, LANES), 0) <= lax.broadcasted_iota(i32, (LANES, LANES), 1), 1.0, 0.0
    ).astype(bf16)
    upto = dot(present.astype(bf16), tri)
    below = jnp.where(
        lax.broadcasted_iota(i32, (his, his), 0) > lax.broadcasted_iota(i32, (his, his), 1), 1.0, 0.0
    ).astype(bf16)
    totals = jnp.broadcast_to(upto[:, LANES - 1 :], (his, LANES))
    rank = upto - present + dot(below, totals.astype(bf16))
    rank_cols = jnp.where(present > 0.5, rank, -1.0).T
    lane = lax.broadcasted_iota(i32, (LANES, LANES), 1).astype(f32)
    sub = lax.broadcasted_iota(i32, (LANES, LANES), 0).astype(f32)
    listed = jnp.zeros((LANES, LANES), f32)
    for h in range(his):
        listed = listed + jnp.where(rank_cols[:, h : h + 1] == lane, sub + float(h * LANES), 0.0)
    list_ref[...] = jnp.sum(listed, axis=0, keepdims=True).astype(i32)

    rank_b = rank.astype(bf16)
    own_iota = lax.broadcasted_iota(i32, (groups, samples), 0)
    for f in range(fields):
        wsum = w_ref[f, 0:1, :]
        for j in range(1, bag_len):
            wsum = wsum + w_ref[f, j : j + 1, :]
        u_map = jnp.full((groups, samples), -1.0, f32)
        c_map = jnp.zeros((groups, samples), f32)
        for j in range(bag_len):
            lo, hi = marks(loc_ref[f, j : j + 1, :])
            u = jnp.sum(dot(rank_b, lo) * hi, axis=0, keepdims=True)
            here = own_iota == own_ref[f, j : j + 1, :]
            u_map = jnp.where(here, u, u_map)
            c_map = jnp.where(here, w_ref[f, j : j + 1, :] / wsum, c_map)
        u_ref[:, f * samples : (f + 1) * samples] = u_map
        c_ref[:, f * samples : (f + 1) * samples] = c_map


def index_call(own, loc, w, groups):
    fields, _, samples = own.shape
    bags = fields * samples
    return pl.pallas_call(
        index_kernel,
        out_shape=(
            jax.ShapeDtypeStruct((1, LANES), i32),
            jax.ShapeDtypeStruct((groups, bags), f32),
            jax.ShapeDtypeStruct((groups, bags), f32),
        ),
        compiler_params=params(),
    )(own, loc, w)


def take_kernel(list_ref, table_ref, out_ref, tb_ref):
    @pl.when(pl.program_id(0) == 0)
    def _():
        tb_ref[...] = table_ref[...].astype(bf16)

    n = list_ref.shape[1]
    rows = table_ref.shape[0]
    asked = jnp.broadcast_to(list_ref[...], (8, n)).T[:, :1]
    marks = jnp.where(lax.broadcasted_iota(i32, (n, rows), 1) == asked, 1.0, 0.0).astype(bf16)
    out_ref[...] = dot(marks, tb_ref[...]).astype(bf16)


def take_call(lists, table):
    n = lists.shape[1]
    rows, width = table.shape
    block = 512 if n % 512 == 0 else n
    return pl.pallas_call(
        take_kernel,
        grid=(n // block,),
        in_specs=[
            pl.BlockSpec((1, block), lambda i: (0, i)),
            pl.BlockSpec((rows, width), lambda i: (0, 0)),
        ],
        out_specs=pl.BlockSpec((block, width), lambda i: (i, 0)),
        out_shape=jax.ShapeDtypeStruct((n, width), bf16),
        scratch_shapes=[pltpu.VMEM((rows, width), bf16)],
        compiler_params=params(("arbitrary",)),
    )(lists, table)


def build(u_ref, c_ref, a_ref, fields, samples, per_step):
    iota = lax.broadcasted_iota(i32, (UNIQ, samples), 0).astype(f32)
    for f in range(fields):
        cols = slice(f * samples, (f + 1) * samples)
        for o in range(0, per_step, 2):
            pair = [
                jnp.where(iota == u_ref[o + k : o + k + 1, cols], c_ref[o + k : o + k + 1, cols], 0.0)
                for k in range(2)
            ]
            a_ref[o * UNIQ : (o + 2) * UNIQ, cols] = jnp.concatenate(pair, axis=0).astype(bf16)


def pool_kernel(fields, u_ref, c_ref, r_ref, x_ref, a_ref, acc_ref):
    per_step, bags = u_ref.shape
    samples = bags // fields
    width = r_ref.shape[1]

    @pl.when(pl.program_id(0) == 0)
    def _():
        acc_ref[...] = jnp.zeros_like(acc_ref)

    build(u_ref, c_ref, a_ref, fields, samples, per_step)
    rt = r_ref[...].astype(f32).T.astype(bf16)
    for f in range(fields):
        cols = slice(f * samples, (f + 1) * samples)
        acc_ref[:, cols] += dot(rt, a_ref[:, cols])

    @pl.when(pl.program_id(0) == pl.num_programs(0) - 1)
    def _():
        for f in range(fields):
            x_ref[:, f * width : (f + 1) * width] = acc_ref[:, f * samples : (f + 1) * samples].T.astype(bf16)


def pool_call(u, c, r, fields):
    groups, bags = u.shape
    width = r.shape[1]
    per_step = min(8, groups)
    return pl.pallas_call(
        functools.partial(pool_kernel, fields),
        grid=(groups // per_step,),
        in_specs=[
            pl.BlockSpec((per_step, bags), lambda i: (i, 0)),
            pl.BlockSpec((per_step, bags), lambda i: (i, 0)),
            pl.BlockSpec((per_step * UNIQ, width), lambda i: (i, 0)),
        ],
        out_specs=pl.BlockSpec((bags // fields, fields * width), lambda i: (0, 0)),
        out_shape=jax.ShapeDtypeStruct((bags // fields, fields * width), bf16),
        scratch_shapes=[
            pltpu.VMEM((per_step * UNIQ, bags), bf16),
            pltpu.VMEM((width, bags), f32),
        ],
        compiler_params=params(("arbitrary",)),
    )(u, c, r)


def head_kernel(x_ref, lab_ref, wa_ref, wb_ref, dt_ref, d_ref, pre_ref, acc_ref):
    samples, ins = x_ref.shape
    parts, _, cut = wa_ref.shape
    width = d_ref.shape[1]
    blocks = [(ref, p) for ref in (wa_ref, wb_ref) for p in range(parts)]
    x = x_ref[...]
    logits = jnp.zeros((samples, 1), f32)
    for k, (ref, p) in enumerate(blocks):
        pre = dot(x, ref[p, :ins, :]) + ref[p, ins : ins + 1, :].astype(f32)
        pre_ref[k] = pre
        out = ref[p, ins + 1 : ins + 2, :].astype(f32)
        logits = logits + jnp.sum(pre * jax.nn.sigmoid(pre) * out, axis=1, keepdims=True)
    labels = jnp.broadcast_to(lab_ref[...], (8, samples)).T[:, :1]
    grad = jax.nn.sigmoid(logits) - labels
    for k, (ref, p) in enumerate(blocks):
        pre = pre_ref[k]
        sig = jax.nn.sigmoid(pre)
        out = ref[p, ins + 1 : ins + 2, :].astype(f32)
        dh = (grad * out * (sig * (1.0 + pre * (1.0 - sig)))).astype(bf16)
        part = dot(ref[p, :ins, :], dh, ((1,), (1,)))
        acc_ref[...] = part if k == 0 else acc_ref[...] + part
    for f in range(ins // width):
        block = acc_ref[f * width : (f + 1) * width, :]
        dt_ref[f * width : (f + 1) * width, :] = block.astype(bf16)
        d_ref[f * samples : (f + 1) * samples, :] = block.T.astype(bf16)


def head_call(x, labels, wa, wb, width):
    samples, ins = x.shape
    parts, _, cut = wa.shape
    return pl.pallas_call(
        head_kernel,
        out_shape=(
            jax.ShapeDtypeStruct((ins, samples), bf16),
            jax.ShapeDtypeStruct((ins // width * samples, width), bf16),
        ),
        scratch_shapes=[
            pltpu.VMEM((2 * parts, samples, cut), f32),
            pltpu.VMEM((ins, samples), f32),
        ],
        compiler_params=params(),
    )(x, labels, wa, wb)


def give_kernel(fields, u_ref, c_ref, d_ref, g_ref, a_ref):
    per_step, bags = u_ref.shape
    build(u_ref, c_ref, a_ref, fields, bags // fields, per_step)
    g_ref[...] = dot(a_ref[...], d_ref[...]).astype(bf16)


def give_call(u, c, d, fields):
    groups, bags = u.shape
    width = d.shape[1]
    per_step = min(8, groups)
    return pl.pallas_call(
        functools.partial(give_kernel, fields),
        grid=(groups // per_step,),
        in_specs=[
            pl.BlockSpec((per_step, bags), lambda i: (i, 0)),
            pl.BlockSpec((per_step, bags), lambda i: (i, 0)),
            pl.BlockSpec((bags, width), lambda i: (0, 0)),
        ],
        out_specs=pl.BlockSpec((per_step * UNIQ, width), lambda i: (i, 0)),
        out_shape=jax.ShapeDtypeStruct((groups * UNIQ, width), bf16),
        scratch_shapes=[pltpu.VMEM((per_step * UNIQ, bags), bf16)],
        compiler_params=params(("arbitrary",)),
    )(u, c, d)


def along_kernel(own_ref, w_ref, u_ref, r_ref, dt_ref, out_ref, acc_ref):
    fields, bag_len, samples = own_ref.shape
    per_step = u_ref.shape[0]
    width = r_ref.shape[1]
    step = pl.program_id(0)

    @pl.when(step == 0)
    def _():
        acc_ref[...] = jnp.zeros_like(acc_ref)

    iota = lax.broadcasted_iota(i32, (UNIQ, samples), 0).astype(f32)
    for f in range(fields):
        cols = slice(f * samples, (f + 1) * samples)
        prod = dot(r_ref[...], dt_ref[f * width : (f + 1) * width, :])
        own = own_ref[f]
        got = acc_ref[f]
        for o in range(per_step):
            hit = jnp.where(iota == u_ref[o : o + 1, cols], prod[o * UNIQ : (o + 1) * UNIQ, :], 0.0)
            value = jnp.sum(hit, axis=0, keepdims=True)
            got = jnp.where(own == step * per_step + o, value, got)
        acc_ref[f] = got

    @pl.when(step == pl.num_programs(0) - 1)
    def _():
        for f in range(fields):
            w = w_ref[f]
            wsum = jnp.sum(w, axis=0, keepdims=True)
            along = acc_ref[f]
            centre = jnp.sum(w * along, axis=0, keepdims=True) / wsum
            out_ref[f] = (along - centre) / wsum


def along_call(own, w, u, r, dt):
    groups, bags = u.shape
    width = r.shape[1]
    per_step = min(8, groups)
    whole3 = pl.BlockSpec(own.shape, lambda i: (0, 0, 0))
    return pl.pallas_call(
        along_kernel,
        grid=(groups // per_step,),
        in_specs=[
            whole3,
            whole3,
            pl.BlockSpec((per_step, bags), lambda i: (i, 0)),
            pl.BlockSpec((per_step * UNIQ, width), lambda i: (i, 0)),
            pl.BlockSpec(dt.shape, lambda i: (0, 0)),
        ],
        out_specs=whole3,
        out_shape=jax.ShapeDtypeStruct(own.shape, f32),
        scratch_shapes=[pltpu.VMEM(own.shape, f32)],
        compiler_params=params(("arbitrary",)),
    )(own, w, u, r, dt)


def add_kernel(list_ref, g_ref, out_ref, acc_ref):
    rows = out_ref.shape[0]
    n = list_ref.shape[1]
    marks = jnp.where(lax.broadcasted_iota(i32, (rows, n), 0) == list_ref[...], 1.0, 0.0).astype(bf16)
    part = dot(marks, g_ref[...])

    @pl.when(pl.program_id(0) == 0)
    def _():
        acc_ref[...] = part

    @pl.when(pl.program_id(0) > 0)
    def _():
        acc_ref[...] += part

    @pl.when(pl.program_id(0) == pl.num_programs(0) - 1)
    def _():
        out_ref[...] = acc_ref[...].astype(bf16)


def add_call(lists, g, rows):
    n = lists.shape[1]
    width = g.shape[1]
    block = 512 if n % 512 == 0 else n
    return pl.pallas_call(
        add_kernel,
        grid=(n // block,),
        in_specs=[
            pl.BlockSpec((1, block), lambda i: (0, i)),
            pl.BlockSpec((block, width), lambda i: (i, 0)),
        ],
        out_specs=pl.BlockSpec((rows, width), lambda i: (0, 0)),
        out_shape=jax.ShapeDtypeStruct((rows, width), bf16),
        scratch_shapes=[pltpu.VMEM((rows, width), f32)],
        compiler_params=params(("arbitrary",)),
    )(lists, g)


def local(owners, local_rows, weights, labels, table, accum, w_in, b_in, w_out):
    samples, fields, bag_len = owners.shape
    rows, width = table.shape
    groups = lax.axis_size("owner")
    dense = lax.axis_size("dense")

    core = lax.axis_index("owner") % 2
    half = w_in.shape[1] // 2
    tail = jnp.zeros((14, w_in.shape[1]), bf16)
    head = jnp.concatenate([w_in, b_in[None], w_out[None], tail], axis=0)
    mine = lax.dynamic_slice_in_dim(head, core * half, half, axis=1)
    wa = lax.all_gather(mine, "dense", axis=0, tiled=False)
    wb = lax.ppermute(wa, "owner", [(i, i ^ 1) for i in range(groups)])

    own = owners.transpose(1, 2, 0)
    w = weights.transpose(1, 2, 0)
    listed, u, c = index_call(own, local_rows.transpose(1, 2, 0), w, groups)
    lists = lax.all_gather(listed[0, :UNIQ], "owner", axis=0, tiled=True)[None]
    found = take_call(lists, table)
    r = lax.all_to_all(found.reshape(groups, UNIQ, width), "owner", split_axis=0, concat_axis=0, tiled=True)
    r = r.reshape(groups * UNIQ, width)
    x = pool_call(u, c, r, fields)
    dt, d = head_call(x, labels.astype(f32)[None], wa, wb, width)
    g = give_call(u, c, d, fields)
    got = lax.all_to_all(g.reshape(groups, UNIQ, width), "owner", split_axis=0, concat_axis=0, tiled=True)
    weight_grad = along_call(own, w, u, r, dt).transpose(2, 0, 1)
    part = add_call(lists, got.reshape(groups * UNIQ, width), rows)
    pieces = lax.all_to_all(part.reshape(dense, rows // dense, width), "dense", split_axis=0, concat_axis=0, tiled=True)
    summed = jnp.sum(pieces.astype(f32), axis=0).astype(bf16)
    row_grad = lax.all_gather(summed, "dense", axis=0, tiled=True).astype(f32)
    new_accum = accum + jnp.mean(row_grad * row_grad, axis=-1)
    new_table = table - step_size * row_grad / jnp.sqrt(new_accum)[:, None]
    return (new_table, new_accum, weight_grad)


def solution(mesh):
    placed = (
        P(("owner", "dense"), None, None),
        P(("owner", "dense"), None, None),
        P(("owner", "dense"), None, None),
        P(("owner", "dense")),
        P("owner", None),
        P("owner"),
        P(None, "dense"),
        P("dense"),
        P("dense"),
    )
    return jax.shard_map(
        local,
        mesh=mesh,
        in_specs=placed,
        out_specs=(P("owner", None), P("owner"), P(("owner", "dense"), None, None)),
        check_vma=False,
    )
```

time: 1090 us -> 569 us (0.52); the launches traced: 1070 us -> 567 us
  waiting for transfers between devices: 472 us -> 119 us
  other arithmetic: 271 us -> 2.91 us
  blocking collectives: 39 us -> 306 us
  local copies, waits for them, and re-layouts: 241 us -> 18.3 us
  Pallas kernels: 0 us -> 90.7 us
  matrix products: 19.3 us -> 0 us
    all_to_all x2, waiting for transfers between devices: 297 us -> 42.1 us  [the longest x1 42.1 us: local(): lax.all_to_all(found.reshape(groups, UNIQ, width), 'owner', split_axis=0,...]
    unnamed x0 -> x1, blocking collectives: none -> 246 us
    scatter-add x1 -> x0, other arithmetic: 145 us -> none  [local(): row_part = jnp.zeros((table_rows, emb_width), jnp.float32).at[asked_piece...]
    gather x2 -> x0, local copies, waits for them, and re-layouts: 143 us -> none  [the longest x1 90.2 us: local(): found_rows = table[asked_piece].astype(jnp.bfloat16)]
    pallas_call x0 -> x7, Pallas kernels: none -> 90.7 us  [the longest x1 15.9 us: take_call(): pl.pallas_call(take_kernel, grid=(n // block,), in_specs=[pl.BlockSpec((1...]
    reduce_scatter x1 -> x0, waiting for transfers between devices: 73 us -> none  [local(): lax.psum_scatter(lax.dot_general(dhidden, w_in, (((1,), (1,)), ((), ())),...]
    psum x1 -> x0, waiting for transfers between devices: 67 us -> none  [local(): lax.psum(row_part.astype(jnp.bfloat16), 'dense').astype(jnp.float32)]
    scatter x1 -> x0, local copies, waits for them, and re-layouts: 50 us -> none  [local(): jnp.zeros((groups * capacity,), jnp.int32).at[slot_place].set(local_flat)]
  transfers between devices with their start and end apart: 5 -> 4, of which waited for: 5 -> 2; matrix products, arithmetic and copies ran while one was open for 1% -> 0% of each run, Pallas kernels for 0% -> 8%
where the time goes in v1:
time: 569 us; the launch traced here: 567 us
  blocking collectives  306 us (54%)
  waiting for transfers between devices  119 us (21%)
  Pallas kernels  90.7 us (16%)
  local copies, waits for them, and re-layouts  18.3 us (3%)
  between operations  14.8 us (3%)
  starting transfers between devices  14.3 us (3%)
    unnamed x1, blocking collectives  246 us
    all_gather x1, waiting for transfers between devices, local(): wa = lax.all_gather(mine, 'dense', axis=0, tiled=False)  77.1 us
    all_to_all x1, blocking collectives, local(): lax.all_to_all(g.reshape(groups, UNIQ, width), 'owner', split_axis=0, con...  48.9 us
    all_to_all x1, waiting for transfers between devices, local(): lax.all_to_all(found.reshape(groups, UNIQ, width), 'owner', split_axis=0,...  42.1 us
    pallas_call x1, Pallas kernels, take_call(): pl.pallas_call(take_kernel, grid=(n // block,), in_specs=[pl.BlockSpec((1...  15.9 us
    pallas_call x1, Pallas kernels, along_call(): pl.pallas_call(along_kernel, grid=(groups // per_step,), in_specs=[whole3...  15 us
    pallas_call x1, Pallas kernels, give_call(): pl.pallas_call(functools.partial(give_kernel, fields), grid=(groups // pe...  14.9 us
    pallas_call x1, Pallas kernels, head_call(): pl.pallas_call(head_kernel, out_shape=(jax.ShapeDtypeStruct((ins, samples...  14.8 us
  transfers between devices with their start and end apart: 4, of which 2 were waited for; matrix products, arithmetic and copies ran while one was open for 0% of the time, Pallas kernels for 8%

profile of v1, /device:TPU:1, one launch (start us, length us, event | category | flops | bytes accessed | tf_op | source)
XLA Modules:
  0.0 566.6 jit_solution(10462374967917842029)
XLA Ops:
  7.2 0.0 all-gather.4.cloned.1.call-start
  7.2 0.7 broadcast_in_dim.21
  7.9 0.7 broadcast_in_dim.22
  8.6 12.3 %concatenate.3 = bf16[1680,1024]{1,0:T(8,128)(2,1)S(1)} concatenate(bf16[1664,1024]{1,0:T(8,128)(2,1)} %param.15, bf16[1,1024]{1,0:T(2,128)(2,1)S(1)} %broadcast_in_dim.21, bf16[1,1024]{1,0:T(2,128)(2,1)S(1)} %broadcast_in_dim.22, bf16[14,1024]{1,0:T(8,128)(2,1)S(1)} %broadcast_in_dim.23), dimensions={0} | concatenate | bytes 6881280 | tf_op jit(solution)/shard_map/concatenate | solution.py:347
  21.0 1.4 constant_dynamic-slice_fusion
  22.4 0.0 all-gather.4.cloned.1.call-update
  22.4 77.1 %all-gather.4.cloned.1.call-done = bf16[6720,512]{1,0:T(8,128)(2,1)} async-done(((bf16[1680,512]{1,0:T(8,128)(2,1)}), bf16[6720,512]{1,0:T(8,128)(2,1)}) %all-gather.4.cloned.1.call-update) | async-done | bytes 6881296 | tf_op jit(solution)/shard_map/all_gather | solution.py:349
  99.5 0.7 collective-permute-start
  100.2 0.6 dynamic-slice
  101.5 5.6 shard_map.112
  107.1 0.7 bitcast_dynamic-update-slice_fusion
  107.9 246.0 %all-reduce = s32[6656]{0:T(1024)S(1)} all-reduce(s32[6656]{0:T(1024)S(1)} %bitcast_dynamic-update-slice_fusion), channel_id=2, replica_groups=mesh['owner'=64,'dense'=4] {'owner'}, use_global_device_ids=true, to_apply=%add | all-reduce | flops 6656 | bytes 53248
  353.9 0.6 reshape.33.list_ref
  354.5 15.9 %shard_map.113 = bf16[6656,128]{1,0:T(8,128)(2,1)} custom-call(s32[1,6656]{1,0:T(1,128)} %reshape.33.list_ref, f32[2048,128]{1,0:T(8,128)} %table_ref.1), custom_call_target="tpu_custom_call" | custom-call | tf_op jit(solution)/shard_map/pallas_call | solution.py:109
  370.4 9.9 %all-to-all-start = ((bf16[64,104,128]{2,1,0:T(8,128)(2,1)}), bf16[64,104,128]{2,1,0:T(8,128)(2,1)S(1)}, u32[]{:S(2)}, u32[]{:S(2)}) async-start(bf16[64,104,128]{2,1,0:T(8,128)(2,1)} %bitcast.18), calls=%async_computation | async-start | bytes 3407872 | tf_op jit(solution)/shard_map/all_to_all | solution.py:357
  380.3 0.6 broadcast_in_dim.24
  380.8 42.1 %all-to-all-done = bf16[64,104,128]{2,1,0:T(8,128)(2,1)S(1)} async-done(((bf16[64,104,128]{2,1,0:T(8,128)(2,1)}), bf16[64,104,128]{2,1,0:T(8,128)(2,1)S(1)}, u32[]{:S(2)}, u32[]{:S(2)}) %all-to-all-start) | async-done | bytes 1703968 | tf_op jit(solution)/shard_map/all_to_all | solution.py:357
  422.9 1.2 copy-done
  424.1 11.5 %shard_map.114.x_ref = bf16[256,1664]{1,0:T(8,128)(2,1)} custom-call(f32[64,3328]{1,0:T(8,128)} %get-tuple-element.9.u_ref, f32[64,3328]{1,0:T(8,128)} %get-tuple-element.10.c_ref, bf16[6656,128]{1,0:T(8,128)(2,1)} %bitcast.14), custom_call_target="tpu_custom_call" | custom-call | tf_op jit(solution)/shard_map/pallas_call | solution.py:160
  435.6 0.0 collective-permute-done.wb_ref
  435.6 14.8 %shard_map.115 = (bf16[1664,256]{1,0:T(8,128)(2,1)}, bf16[3328,128]{1,0:T(8,128)(2,1)}) custom-call(bf16[256,1664]{1,0:T(8,128)(2,1)} %shard_map.114.x_ref, f32[1,256]{1,0:T(1,128)} %bitcast.28, bf16[4,1680,512]{2,1,0:T(8,128)(2,1)} %bitcast.17, bf16[4,1680,512]{2,1,0:T(8,128)(2,1)} %collective-permute-done.wb_ref), custom_call_target="tpu_custom_call" | custom-call | tf_op jit(solution)/shard_map/pallas_call | solution.py:208
  450.4 14.9 %shard_map.116 = bf16[6656,128]{1,0:T(8,128)(2,1)} custom-call(f32[64,3328]{1,0:T(8,128)} %get-tuple-element.9.u_ref, f32[64,3328]{1,0:T(8,128)} %get-tuple-element.10.c_ref, bf16[3328,128]{1,0:T(8,128)(2,1)} %get-tuple-element.11.d_ref), custom_call_target="tpu_custom_call" | custom-call | tf_op jit(solution)/shard_map/pallas_call | solution.py:232
  465.3 48.9 %all_to_all.15 = bf16[64,104,128]{2,1,0:T(8,128)(2,1)} all-to-all(bf16[64,104,128]{2,1,0:T(8,128)(2,1)} %bitcast.20), channel_id=1, replica_groups=mesh['owner'=64,'dense'=4] {'owner'}, dimensions={0} | all-to-all | bytes 3407872 | tf_op jit(solution)/shard_map/all_to_all | solution.py:362
  514.1 13.0 %shard_map.117 = bf16[2048,128]{1,0:T(8,128)(2,1)} custom-call(s32[1,6656]{1,0:T(1,128)} %reshape.33.list_ref, bf16[6656,128]{1,0:T(8,128)(2,1)} %bitcast.19), custom_call_target="tpu_custom_call" | custom-call | tf_op jit(solution)/shard_map/pallas_call | solution.py:324
  527.1 3.7 all-to-all-start.2
  530.8 15.0 %shard_map.118 = f32[13,4,256]{2,1,0:T(4,128)} custom-call(s32[13,4,256]{2,1,0:T(4,128)} %bitcast.23, f32[13,4,256]{2,1,0:T(4,128)} %bitcast.25, f32[64,3328]{1,0:T(8,128)} %get-tuple-element.9.u_ref, bf16[6656,128]{1,0:T(8,128)(2,1)} %bitcast.15, bf16[1664,256]{1,0:T(8,128)(2,1)} %get-tuple-element.12.dt_ref), custom_call_target="tpu_custom_call" | custom-call | tf_op jit(solution)/shard_map/pallas_call | solution.py:284
  545.9 0.0 all-to-all-done.2
  545.9 0.1 reduce_sum.21
  546.0 11.5 %all_gather.15 = bf16[2048,128]{1,0:T(8,128)(2,1)S(1)} all-gather(bf16[512,128]{1,0:T(8,128)(2,1)S(1)} %reduce_sum.21), channel_id=1, replica_groups=mesh['owner'=64,'dense'=4] {'dense'}, dimensions={0}, use_global_device_ids=true | all-gather | bytes 655360 | tf_op jit(solution)/shard_map/all_gather | solution.py:367
  557.5 0.3 fusion.2
  557.8 0.6 fusion.3
  558.4 1.3 fusion.1
  (11 shorter events, 0.0 us)
Async XLA Ops:
  7.2 92.4 %all-gather.4.cloned.1.call-start = ((), (), s32[]{:S(2)}) async-start(), calls=%async_computation.3 | async-start | bytes 8601600 | tf_op jit(solution)/shard_map/all_gather | solution.py:349
  22.4 77.8 %copy-start.4 = (u32[256]{0:T(256)S(1)}, u32[256]{0:T(256)}, u32[]{:S(2)}) copy-start(u32[256]{0:T(256)} %constant.36) | copy-start | bytes 3076
  99.5 336.1 %collective-permute-start = (bf16[4,1680,512]{2,1,0:T(8,128)(2,1)}, bf16[4,1680,512]{2,1,0:T(8,128)(2,1)}, u32[]{:S(2)}, u32[]{:S(2)}) collective-permute-start(bf16[4,1680,512]{2,1,0:T(8,128)(2,1)} %bitcast.16), channel_id=1, source_target_pairs={{0,4},{4,0},{8,12},{12,8},{16,20},{20,16},{24,28},{28,24},{32,36},... | collective-permute-start | bytes 20643848 | tf_op jit(solution)/shard_map/ppermute | solution.py:350
  370.4 9.9 %copy-start.3 = (bf16[256]{0:T(256)(128)(2,1)S(1)}, bf16[256]{0:T(256)(128)(2,1)}, u32[]{:S(2)}) copy-start(bf16[256]{0:T(256)(128)(2,1)} %param.12) | copy-start | bytes 1540
  370.4 52.5 %all-to-all-start = ((bf16[64,104,128]{2,1,0:T(8,128)(2,1)}), bf16[64,104,128]{2,1,0:T(8,128)(2,1)S(1)}, u32[]{:S(2)}, u32[]{:S(2)}) async-start(bf16[64,104,128]{2,1,0:T(8,128)(2,1)} %bitcast.18), calls=%async_computation | async-start | bytes 3407872 | tf_op jit(solution)/shard_map/all_to_all | solution.py:357
  422.9 1.2 copy-start
  527.1 18.8 %all-to-all-start.2 = ((bf16[4,512,128]{2,1,0:T(8,128)(2,1)}), bf16[4,512,128]{2,1,0:T(8,128)(2,1)S(1)}, u32[]{:S(2)}, u32[]{:S(2)}) async-start(bf16[4,512,128]{2,1,0:T(8,128)(2,1)} %bitcast.21), calls=%async_computation.2 | async-start | bytes 1048576 | tf_op jit(solution)/shard_map/all_to_all | solution.py:365
  545.9 12.0 %copy-start.2 = (f32[2048]{0:T(1024)S(1)}, f32[2048]{0:T(1024)}, u32[]{:S(2)}) copy-start(f32[2048]{0:T(1024)} %param.14) | copy-start | bytes 24580
  545.9 12.6 %copy-start.1 = (f32[2048,128]{1,0:T(8,128)S(1)}, f32[2048,128]{1,0:T(8,128)}, u32[]{:S(2)}) copy-start(f32[2048,128]{1,0:T(8,128)} %table_ref.1) | copy-start | bytes 3145732
Sparse Core Ops, SparseCore 0:
  22.5 76.9 all-gather.3

commit v2 on v1

v2 whole, which is shorter than its diff:
```python
import functools

import jax
import jax.numpy as jnp
from jax import lax
from jax.experimental import pallas as pl
from jax.experimental.pallas import tpu as pltpu
from jax.sharding import PartitionSpec as P

step_size = 0.5
UNIQ = 104
ROWS_DEV = 2048
LANES = 128
CHUNKS = ((0, 48), (48, 104))
TAIL = 16
VMEM_LIMIT = 56 * 1024 * 1024
f32, bf16, i32 = jnp.float32, jnp.bfloat16, jnp.int32


def dot(a, b, dims=((1,), (0,))):
    return lax.dot_general(a, b, (dims, ((), ())), preferred_element_type=f32)


def params(sem=None):
    return pltpu.CompilerParams(vmem_limit_bytes=VMEM_LIMIT, dimension_semantics=sem)


def cost(flops, moved=1 << 20):
    return pl.CostEstimate(flops=1 << 20, bytes_accessed=1 << 10, transcendentals=0)


def after(x, *before):
    return lax.optimization_barrier((x, *before))[0]


def marks_of(row, samples):
    lo = lax.broadcasted_iota(i32, (LANES, samples), 0) == (row & (LANES - 1))
    hi = lax.broadcasted_iota(i32, (ROWS_DEV // LANES, samples), 0) == (row >> 7)
    return jnp.where(lo, 1.0, 0.0).astype(bf16), jnp.where(hi, 1.0, 0.0)


def list_kernel(loc_ref, list_ref, rank_ref):
    fields, bag_len, samples = loc_ref.shape
    his = ROWS_DEV // LANES
    count = jnp.zeros((his, LANES), f32)
    for f in range(fields):
        for j in range(bag_len):
            lo, hi = marks_of(loc_ref[f, j : j + 1, :], samples)
            count = count + dot(hi.astype(bf16), lo, ((1,), (1,)))
    present = jnp.where(count > 0.5, 1.0, 0.0)
    tri = jnp.where(
        lax.broadcasted_iota(i32, (LANES, LANES), 0) <= lax.broadcasted_iota(i32, (LANES, LANES), 1), 1.0, 0.0
    ).astype(bf16)
    upto = dot(present.astype(bf16), tri)
    below = jnp.where(
        lax.broadcasted_iota(i32, (his, his), 0) > lax.broadcasted_iota(i32, (his, his), 1), 1.0, 0.0
    ).astype(bf16)
    totals = jnp.broadcast_to(upto[:, LANES - 1 :], (his, LANES))
    rank = upto - present + dot(below, totals.astype(bf16))
    rank_ref[...] = rank
    rank_cols = jnp.where(present > 0.5, rank, -1.0).T
    lane = lax.broadcasted_iota(i32, (LANES, LANES), 1).astype(f32)
    sub = lax.broadcasted_iota(i32, (LANES, LANES), 0).astype(f32)
    listed = jnp.zeros((LANES, LANES), f32)
    for h in range(his):
        listed = listed + jnp.where(rank_cols[:, h : h + 1] == lane, sub + float(h * LANES), 0.0)
    row = jnp.sum(listed, axis=0, keepdims=True).astype(i32)
    list_ref[...] = jnp.broadcast_to(row, list_ref.shape)


def list_call(loc, groups):
    return pl.pallas_call(
        list_kernel,
        out_shape=(
            jax.ShapeDtypeStruct((groups, LANES), i32),
            jax.ShapeDtypeStruct((ROWS_DEV // LANES, LANES), f32),
        ),
        compiler_params=params(),
        cost_estimate=cost(1 << 31),
    )(loc)


def map_kernel(own_ref, loc_ref, w_ref, rank_ref, u_ref, c_ref):
    fields, bag_len, samples = own_ref.shape
    groups = u_ref.shape[0]
    rank_b = rank_ref[...].astype(bf16)
    own_iota = lax.broadcasted_iota(i32, (groups, samples), 0)
    for f in range(fields):
        wsum = w_ref[f, 0:1, :]
        for j in range(1, bag_len):
            wsum = wsum + w_ref[f, j : j + 1, :]
        u_map = jnp.full((groups, samples), -1.0, f32)
        c_map = jnp.zeros((groups, samples), f32)
        for j in range(bag_len):
            lo, hi = marks_of(loc_ref[f, j : j + 1, :], samples)
            u = jnp.sum(dot(rank_b, lo) * hi, axis=0, keepdims=True)
            here = own_iota == own_ref[f, j : j + 1, :]
            u_map = jnp.where(here, u, u_map)
            c_map = jnp.where(here, w_ref[f, j : j + 1, :] / wsum, c_map)
        u_ref[:, f * samples : (f + 1) * samples] = u_map
        c_ref[:, f * samples : (f + 1) * samples] = c_map


def map_call(own, loc, w, rank, groups):
    fields, _, samples = own.shape
    bags = fields * samples
    return pl.pallas_call(
        map_kernel,
        out_shape=(
            jax.ShapeDtypeStruct((groups, bags), f32),
            jax.ShapeDtypeStruct((groups, bags), f32),
        ),
        compiler_params=params(),
        cost_estimate=cost(1 << 31),
    )(own, loc, w, rank)


def half_kernel(core_ref, w_ref, b_ref, o_ref, out_ref):
    ins = w_ref.shape[0]
    out_ref[:ins, :] = w_ref[...]
    cut = w_ref.shape[1]
    rows = jnp.concatenate(
        [b_ref[...].astype(f32), o_ref[...].astype(f32), jnp.zeros((TAIL - 2, cut), f32)], axis=0
    )
    out_ref[ins:, :] = rows.astype(bf16)


def half_call(core, w_in, b_in, w_out):
    ins, hidden = w_in.shape
    cut = hidden // 2
    return pl.pallas_call(
        half_kernel,
        grid_spec=pltpu.PrefetchScalarGridSpec(
            num_scalar_prefetch=1,
            grid=(1,),
            in_specs=[
                pl.BlockSpec((ins, cut), lambda i, core: (0, core[0])),
                pl.BlockSpec((1, cut), lambda i, core: (0, core[0])),
                pl.BlockSpec((1, cut), lambda i, core: (0, core[0])),
            ],
            out_specs=pl.BlockSpec((ins + TAIL, cut), lambda i, core: (0, 0)),
        ),
        out_shape=jax.ShapeDtypeStruct((ins + TAIL, cut), bf16),
        compiler_params=params(("arbitrary",)),
    )(core, w_in, b_in[None], w_out[None])


def take_kernel(lo, hi, list_ref, tb_ref, out_ref):
    rows = tb_ref.shape[0]
    per_step = list_ref.shape[0]
    asked = list_ref[...].T
    iota = lax.broadcasted_iota(i32, (hi - lo, rows), 1)
    marks = [jnp.where(iota == asked[lo:hi, o : o + 1], 1.0, 0.0) for o in range(per_step)]
    out_ref[...] = dot(jnp.concatenate(marks, axis=0).astype(bf16), tb_ref[...]).astype(bf16)


def take_call(lists, tb, lo, hi):
    groups = lists.shape[0]
    rows, width = tb.shape
    per_step = min(8, groups)
    n = hi - lo
    return pl.pallas_call(
        functools.partial(take_kernel, lo, hi),
        grid=(groups // per_step,),
        in_specs=[
            pl.BlockSpec((per_step, LANES), lambda i: (i, 0)),
            pl.BlockSpec((rows, width), lambda i: (0, 0)),
        ],
        out_specs=pl.BlockSpec((per_step * n, width), lambda i: (i, 0)),
        out_shape=jax.ShapeDtypeStruct((groups * n, width), bf16),
        compiler_params=params(("arbitrary",)),
        cost_estimate=cost(2 * groups * n * rows * width * 2),
    )(lists, tb)


def build(u_ref, c_ref, a_ref, fields, samples, per_step, lo, hi):
    n = hi - lo
    iota = lax.broadcasted_iota(i32, (n, samples), 0).astype(f32) + float(lo)
    for f in range(fields):
        cols = slice(f * samples, (f + 1) * samples)
        for o in range(0, per_step, 2):
            pair = [
                jnp.where(iota == u_ref[o + k : o + k + 1, cols], c_ref[o + k : o + k + 1, cols], 0.0)
                for k in range(2)
            ]
            a_ref[o * n : (o + 2) * n, cols] = jnp.concatenate(pair, axis=0).astype(bf16)


def pool_kernel(fields, lo, hi, last, u_ref, c_ref, r_ref, *refs):
    per_step, bags = u_ref.shape
    samples = bags // fields
    width = r_ref.shape[1]
    prev_ref = refs[0] if last else None
    x_ref, a_ref, acc_ref = refs[-3:] if last else (None, refs[-1], refs[0])

    @pl.when(pl.program_id(0) == 0)
    def _():
        acc_ref[...] = prev_ref[...] if last else jnp.zeros_like(acc_ref)

    build(u_ref, c_ref, a_ref, fields, samples, per_step, lo, hi)
    rt = r_ref[...].astype(f32).T.astype(bf16)
    for f in range(fields):
        cols = slice(f * samples, (f + 1) * samples)
        acc_ref[:, cols] += dot(rt, a_ref[:, cols])

    if last:

        @pl.when(pl.program_id(0) == pl.num_programs(0) - 1)
        def _():
            for f in range(fields):
                x_ref[:, f * width : (f + 1) * width] = acc_ref[:, f * samples : (f + 1) * samples].T.astype(bf16)


def pool_call(u, c, r, fields, lo, hi, prev, last):
    groups, bags = u.shape
    width = r.shape[1]
    per_step = min(8, groups)
    n = hi - lo
    acc = jax.ShapeDtypeStruct((width, bags), f32)
    x = jax.ShapeDtypeStruct((bags // fields, fields * width), bf16)
    acc_spec = pl.BlockSpec((width, bags), lambda i: (0, 0))
    return pl.pallas_call(
        functools.partial(pool_kernel, fields, lo, hi, last),
        grid=(groups // per_step,),
        in_specs=[
            pl.BlockSpec((per_step, bags), lambda i: (i, 0)),
            pl.BlockSpec((per_step, bags), lambda i: (i, 0)),
            pl.BlockSpec((per_step * n, width), lambda i: (i, 0)),
        ]
        + ([acc_spec] if last else []),
        out_specs=pl.BlockSpec(x.shape, lambda i: (0, 0)) if last else acc_spec,
        out_shape=x if last else acc,
        scratch_shapes=[pltpu.VMEM((per_step * n, bags), bf16)] + ([pltpu.VMEM((width, bags), f32)] if last else []),
        compiler_params=params(("arbitrary",)),
        cost_estimate=cost(2 * groups * n * bags * width * 2),
    )(u, c, r, *([prev] if last else []))


def head_kernel(sides, x_ref, lab_ref, *refs):
    weights, (dt_ref, d_ref, pre_ref, acc_ref), refs = refs[: 5 * sides], refs[5 * sides : 5 * sides + 4], refs[5 * sides + 4 :]
    held, sem = refs[: 5 * sides], refs[5 * sides]
    samples, ins = x_ref.shape
    width = d_ref.shape[1]
    copies = [pltpu.make_async_copy(weights[k], held[k], sem.at[k]) for k in range(5 * sides)]
    for copy in copies:
        copy.start()
    x = x_ref[...]
    top = held[3].shape[0]
    logits = jnp.zeros((samples, 1), f32)
    blocks = [(5 * s + p,) for s in range(sides) for p in range(3)] + [(5 * s + 3, 5 * s + 4) for s in range(sides)]

    def tail(block):
        ref = held[block[-1]]
        at = ins if len(block) == 1 else ins - top
        return ref[at : at + 1, :].astype(f32), ref[at + 1 : at + 2, :].astype(f32)

    for k, block in enumerate(blocks):
        for b in block:
            copies[b].wait()
        bias, out = tail(block)
        if len(block) == 1:
            pre = dot(x, held[block[0]][:ins, :]) + bias
        else:
            pre = dot(x[:, :top], held[block[0]][...]) + dot(x[:, top:], held[block[1]][: ins - top, :]) + bias
        pre_ref[k] = pre
        logits = logits + jnp.sum(pre * jax.nn.sigmoid(pre) * out, axis=1, keepdims=True)
    labels = jnp.broadcast_to(lab_ref[...], (8, samples)).T[:, :1]
    grad = jax.nn.sigmoid(logits) - labels
    for k, block in enumerate(blocks):
        pre = pre_ref[k]
        sig = jax.nn.sigmoid(pre)
        out = tail(block)[1]
        dh = (grad * out * (sig * (1.0 + pre * (1.0 - sig)))).astype(bf16)
        if len(block) == 1:
            part = dot(held[block[0]][:ins, :], dh, ((1,), (1,)))
            acc_ref[...] = part if k == 0 else acc_ref[...] + part
        else:
            acc_ref[:top, :] += dot(held[block[0]][...], dh, ((1,), (1,)))
            acc_ref[top:, :] += dot(held[block[1]][: ins - top, :], dh, ((1,), (1,)))
    for f in range(ins // width):
        block = acc_ref[f * width : (f + 1) * width, :]
        dt_ref[f * width : (f + 1) * width, :] = block.astype(bf16)
        d_ref[f * samples : (f + 1) * samples, :] = block.T.astype(bf16)


def head_call(x, labels, weights, width):
    samples, ins = x.shape
    sides = len(weights) // 5
    cut = weights[0].shape[1]
    n = len(weights)
    vmem = pl.BlockSpec(memory_space=pltpu.VMEM)
    return pl.pallas_call(
        functools.partial(head_kernel, sides),
        in_specs=[vmem, vmem] + [pl.BlockSpec(memory_space=pl.ANY)] * n,
        out_specs=(vmem, vmem),
        out_shape=(
            jax.ShapeDtypeStruct((ins, samples), bf16),
            jax.ShapeDtypeStruct((ins // width * samples, width), bf16),
        ),
        scratch_shapes=[
            pltpu.VMEM((4 * sides, samples, cut), f32),
            pltpu.VMEM((ins, samples), f32),
        ]
        + [pltpu.VMEM(a.shape, bf16) for a in weights]
        + [pltpu.SemaphoreType.DMA((n,))],
        compiler_params=params(),
        cost_estimate=cost(4 * samples * ins * cut * 4 * sides, 14 << 20),
    )(x, labels, *weights)


def give_kernel(fields, lo, hi, u_ref, c_ref, d_ref, g_ref, a_ref):
    per_step, bags = u_ref.shape
    build(u_ref, c_ref, a_ref, fields, bags // fields, per_step, lo, hi)
    g_ref[...] = dot(a_ref[...], d_ref[...]).astype(bf16)


def give_call(u, c, d, fields, lo, hi):
    groups, bags = u.shape
    width = d.shape[1]
    per_step = min(8, groups)
    n = hi - lo
    return pl.pallas_call(
        functools.partial(give_kernel, fields, lo, hi),
        grid=(groups // per_step,),
        in_specs=[
            pl.BlockSpec((per_step, bags), lambda i: (i, 0)),
            pl.BlockSpec((per_step, bags), lambda i: (i, 0)),
            pl.BlockSpec((bags, width), lambda i: (0, 0)),
        ],
        out_specs=pl.BlockSpec((per_step * n, width), lambda i: (i, 0)),
        out_shape=jax.ShapeDtypeStruct((groups * n, width), bf16),
        scratch_shapes=[pltpu.VMEM((per_step * n, bags), bf16)],
        compiler_params=params(("arbitrary",)),
        cost_estimate=cost(2 * groups * n * bags * width * 2),
    )(u, c, d)


def along_kernel(own_ref, w_ref, u_ref, dt_ref, *refs):
    r_refs, (out_ref, acc_ref) = refs[:-2], refs[-2:]
    fields, bag_len, samples = own_ref.shape
    per_step = u_ref.shape[0]
    width = r_refs[0].shape[1]
    step = pl.program_id(0)

    @pl.when(step == 0)
    def _():
        acc_ref[...] = jnp.zeros_like(acc_ref)

    for f in range(fields):
        cols = slice(f * samples, (f + 1) * samples)
        d = dt_ref[f * width : (f + 1) * width, :]
        prods = [dot(r_ref[...], d) for r_ref in r_refs]
        own = own_ref[f]
        got = acc_ref[f]
        for o in range(per_step):
            value = None
            for (lo, hi), prod in zip(CHUNKS, prods):
                n = hi - lo
                iota = lax.broadcasted_iota(i32, (n, samples), 0).astype(f32) + float(lo)
                hit = jnp.where(iota == u_ref[o : o + 1, cols], prod[o * n : (o + 1) * n, :], 0.0)
                part = jnp.sum(hit.reshape(n // 8, 8, samples), axis=0)
                value = part if value is None else value + part
            value = jnp.sum(value, axis=0, keepdims=True)
            got = jnp.where(own == step * per_step + o, value, got)
        acc_ref[f] = got

    @pl.when(step == pl.num_programs(0) - 1)
    def _():
        for f in range(fields):
            w = w_ref[f]
            wsum = jnp.sum(w, axis=0, keepdims=True)
            along = acc_ref[f]
            centre = jnp.sum(w * along, axis=0, keepdims=True) / wsum
            out_ref[f] = (along - centre) / wsum


def along_call(own, w, u, dt, rs):
    groups, bags = u.shape
    width = rs[0].shape[1]
    per_step = min(8, groups)
    whole3 = pl.BlockSpec(own.shape, lambda i: (0, 0, 0))
    return pl.pallas_call(
        along_kernel,
        grid=(groups // per_step,),
        in_specs=[
            whole3,
            whole3,
            pl.BlockSpec((per_step, bags), lambda i: (i, 0)),
            pl.BlockSpec(dt.shape, lambda i: (0, 0)),
        ]
        + [pl.BlockSpec((per_step * (hi - lo), width), lambda i: (i, 0)) for lo, hi in CHUNKS],
        out_specs=whole3,
        out_shape=jax.ShapeDtypeStruct(own.shape, f32),
        scratch_shapes=[pltpu.VMEM(own.shape, f32)],
        compiler_params=params(("arbitrary",)),
        cost_estimate=cost(2 * groups * UNIQ * bags * width * 2),
    )(own, w, u, dt, *rs)


def add_kernel(last, list_ref, g_ref, *refs):
    prev_ref = refs[0] if last else None
    out_ref, acc_ref = refs[-2:] if last else (None, refs[0])
    rows = acc_ref.shape[0]
    n = list_ref.shape[1]

    @pl.when(pl.program_id(0) == 0)
    def _():
        acc_ref[...] = prev_ref[...] if last else jnp.zeros_like(acc_ref)

    marks = jnp.where(lax.broadcasted_iota(i32, (rows, n), 0) == list_ref[...], 1.0, 0.0).astype(bf16)
    acc_ref[...] += dot(marks, g_ref[...])

    if last:

        @pl.when(pl.program_id(0) == pl.num_programs(0) - 1)
        def _():
            out_ref[...] = acc_ref[...].astype(bf16)


def add_call(lists, g, rows, prev, last):
    n = lists.shape[1]
    width = g.shape[1]
    block = 512 if n % 512 == 0 else n
    whole = pl.BlockSpec((rows, width), lambda i: (0, 0))
    return pl.pallas_call(
        functools.partial(add_kernel, last),
        grid=(n // block,),
        in_specs=[
            pl.BlockSpec((1, block), lambda i: (0, i)),
            pl.BlockSpec((block, width), lambda i: (i, 0)),
        ]
        + ([whole] if last else []),
        out_specs=whole,
        out_shape=jax.ShapeDtypeStruct((rows, width), bf16 if last else f32),
        scratch_shapes=[pltpu.VMEM((rows, width), f32)] if last else [],
        compiler_params=params(("arbitrary",)),
        cost_estimate=cost(2 * n * rows * width * 2),
    )(lists, g, *([prev] if last else []))


def send(x, groups):
    width = x.shape[1]
    return lax.all_to_all(
        x.reshape(groups, -1, width), "owner", split_axis=0, concat_axis=0, tiled=True
    ).reshape(-1, width)


def turn(x, shift):
    dense = lax.axis_size("dense")
    return lax.ppermute(x, "dense", [(i, (i + shift) % dense) for i in range(dense)])


def swap(x):
    return lax.ppermute(x, "owner", [(i, i ^ 1) for i in range(lax.axis_size("owner"))])


def local(owners, local_rows, weights, labels, table, accum, w_in, b_in, w_out):
    fields = owners.shape[1]
    rows, width = table.shape
    groups = lax.axis_size("owner")
    dense = lax.axis_size("dense")
    own, loc, w = (a.transpose(1, 2, 0) for a in (owners, local_rows, weights))

    mine = half_call((lax.axis_index("owner") % 2).astype(i32)[None], w_in, b_in, w_out)
    ahead, behind = turn(mine, 1), turn(mine, dense - 1)

    listed, rank = list_call(loc, groups)
    lists = lax.all_to_all(listed, "owner", split_axis=0, concat_axis=0, tiled=True)
    u, c = map_call(own, loc, w, rank, groups)
    flat = [lists[:, lo:hi].reshape(1, groups * (hi - lo)) for lo, hi in CHUNKS]
    tb = table.astype(bf16)

    found = [take_call(lists, tb, lo, hi) for lo, hi in CHUNKS]
    rs = [send(x, groups) for x in found]

    cut = (mine.shape[0] // 32) * 16
    ahead, behind = after(ahead, found[-1]), after(behind, found[-1])
    far = [turn(ahead[:cut], 1), turn(behind[cut:], dense - 1)]
    near = [mine, ahead, behind]
    other = [swap(after(a, found[-1])) for a in near]
    far = [after(a, rs[0]) for a in far]
    head_weights = near + far + other + [swap(a) for a in far]

    x = None
    for k, (lo, hi) in enumerate(CHUNKS):
        x = pool_call(u, c, rs[k], fields, lo, hi, x, k == len(CHUNKS) - 1)
    dt, d = head_call(x, labels.astype(f32)[None], head_weights, width)
    gs = [give_call(u, c, d, fields, lo, hi) for lo, hi in CHUNKS]
    gots = [send(g, groups) for g in gs]
    weight_grad = along_call(own, w, u, after(dt, *gs), rs)
    part = None
    for k in range(len(CHUNKS)):
        got = after(gots[k], weight_grad) if k == 0 else gots[k]
        part = add_call(flat[k], got, rows, part, k == len(CHUNKS) - 1)

    cut = rows // dense
    me = lax.axis_index("dense")
    piece = lambda k: lax.dynamic_slice_in_dim(part, lax.rem(me + k, dense) * cut, cut, axis=0)
    total = piece(0).astype(f32)
    for k in range(1, dense):
        total = total + turn(piece(k), k).astype(f32)
    total = total.astype(bf16)
    row_grad = jnp.zeros((rows, width), bf16)
    for k in range(dense):
        got = total if k == 0 else turn(total, k)
        row_grad = lax.dynamic_update_slice_in_dim(row_grad, got, lax.rem(me + dense - k, dense) * cut, axis=0)
    row_grad = row_grad.astype(f32)
    new_accum = accum + jnp.mean(row_grad * row_grad, axis=-1)
    new_table = table - step_size * row_grad / jnp.sqrt(new_accum)[:, None]
    return (new_table, new_accum, weight_grad.transpose(2, 0, 1))


def solution(mesh):
    placed = (
        P(("owner", "dense"), None, None),
        P(("owner", "dense"), None, None),
        P(("owner", "dense"), None, None),
        P(("owner", "dense")),
        P("owner", None),
        P("owner"),
        P(None, "dense"),
        P("dense"),
        P("dense"),
    )
    return jax.shard_map(
        local,
        mesh=mesh,
        in_specs=placed,
        out_specs=(P("owner", None), P("owner"), P(("owner", "dense"), None, None)),
        check_vma=False,
    )
```

time: 569 us -> 254 us (0.45)
  blocking collectives: 306 us -> 0 us
  waiting for transfers between devices: 119 us -> 73.1 us
  starting transfers between devices: 14.3 us -> 54.3 us
  Pallas kernels: 90.7 us -> 107 us
  between operations: 14.8 us -> 0.91 us
  local copies, waits for them, and re-layouts: 18.3 us -> 11.1 us
    unnamed x1 -> x0, blocking collectives: 246 us -> none
    all_gather x1 -> x0, waiting for transfers between devices: 77.1 us -> none  [local(): wa = lax.all_gather(mine, 'dense', axis=0, tiled=False)]
    all_to_all x1 -> x0, blocking collectives: 48.9 us -> none  [local(): lax.all_to_all(g.reshape(groups, UNIQ, width), 'owner', split_axis=0, con...]
    ppermute x1 -> x15, waiting for transfers between devices: 0.01 us -> 34.9 us  [the longest x10 34.9 us: turn(): lax.ppermute(x, 'dense', [(i, (i + shift) % dense) for i in range(dense)])]
    all_to_all x2 -> x5, starting transfers between devices: 13.6 us -> 39.8 us  [the longest x4 27.4 us: send(): lax.all_to_all(x.reshape(groups, -1, width), 'owner', split_axis=0, conca...]
    pallas_call x6 -> x12, Pallas kernels: 75.7 us -> 91 us  [the longest x2 18.8 us: give_call(): pl.pallas_call(functools.partial(give_kernel, fields, lo, hi), grid=(grou...]
    ppermute x1 -> x15, starting transfers between devices: 0.71 us -> 14.5 us  [the longest x10 11.1 us: turn(): lax.ppermute(x, 'dense', [(i, (i + shift) % dense) for i in range(dense)])]
    concatenate x1 -> x0, local copies, waits for them, and re-layouts: 12.3 us -> none  [local(): head = jnp.concatenate([w_in, b_in[None], w_out[None], tail], axis=0)]
  transfers between devices with their start and end apart: 4 -> 20, of which waited for: 2 -> 9; matrix products, arithmetic and copies ran while one was open for 0% -> 2% of each run, Pallas kernels for 8% -> 29%
where the time goes in v2:
time: 254 us; the launch traced here: 251 us
  Pallas kernels  107 us (42%)
  waiting for transfers between devices  73.1 us (29%)
  starting transfers between devices  54.3 us (21%)
  local copies, waits for them, and re-layouts  11.1 us (4%)
  other arithmetic  4.71 us (2%)
    ppermute x10, waiting for transfers between devices, turn(): lax.ppermute(x, 'dense', [(i, (i + shift) % dense) for i in range(dense)])  34.9 us
    all_to_all x4, waiting for transfers between devices, send(): lax.all_to_all(x.reshape(groups, -1, width), 'owner', split_axis=0, conca...  29.8 us
    all_to_all x4, starting transfers between devices, send(): lax.all_to_all(x.reshape(groups, -1, width), 'owner', split_axis=0, conca...  27.4 us
    pallas_call x2, Pallas kernels, give_call(): pl.pallas_call(functools.partial(give_kernel, fields, lo, hi), grid=(grou...  18.8 us
    pallas_call x2, Pallas kernels, pool_call(): pl.pallas_call(functools.partial(pool_kernel, fields, lo, hi, last), grid...  18.5 us
    pallas_call x1, Pallas kernels, along_call(): pl.pallas_call(along_kernel, grid=(groups // per_step,), in_specs=[whole3...  16.2 us
    pallas_call x2, Pallas kernels, take_call(): pl.pallas_call(functools.partial(take_kernel, lo, hi), grid=(groups // pe...  15.3 us
    pallas_call x2, Pallas kernels, add_call(): pl.pallas_call(functools.partial(add_kernel, last), grid=(n // block,), i...  14.5 us
  transfers between devices with their start and end apart: 20, of which 9 were waited for; matrix products, arithmetic and copies ran while one was open for 2% of the time, Pallas kernels for 29%

profile of v2, /device:TPU:1, one launch (start us, length us, event | category | flops | bytes accessed | tf_op | source)
XLA Modules:
  0.0 251.4 jit_solution(9931174763140625186)
XLA Ops:
  3.2 2.9 %shard_map.118.refs_0_ = bf16[1680,512]{1,0:T(8,128)(2,1)} custom-call(s32[1]{0:T(128)} %bitcast.11.core_ref, bf16[1664,1024]{1,0:T(8,128)(2,1)} %w_ref.1, bf16[1,1024]{1,0:T(2,128)(2,1)} %broadcast_in_dim.22.b_ref, bf16[1,1024]{1,0:T(2,128)(2,1)} %broadcast_in_dim.23.o_ref), custom_call_target="tpu_custom_call" | custom-call | tf_op jit(solution)/shard_map/pallas_call | solution.py:131
  6.1 3.6 %collective-permute-start.1 = (bf16[1680,512]{1,0:T(8,128)(2,1)}, bf16[1680,512]{1,0:T(8,128)(2,1)}, u32[]{:S(2)}, u32[]{:S(2)}) collective-permute-start(bf16[1680,512]{1,0:T(8,128)(2,1)} %shard_map.118.refs_0_), channel_id=1, source_target_pairs={{0,3},{1,0},{2,1},{3,2},{4,7},{5,4},{6,5},{7,6},{8,11},{9,8},{10,9... | collective-permute-start | bytes 5160968 | tf_op jit(solution)/shard_map/ppermute | solution.py:450
  9.7 3.3 %shard_map.112 = (s32[64,128]{1,0:T(8,128)}, f32[16,128]{1,0:T(8,128)}) custom-call(s32[13,4,256]{2,1,0:T(4,128)} %bitcast.37), custom_call_target="tpu_custom_call" | custom-call | flops 1048576 | bytes 1024 | tf_op jit(solution)/shard_map/pallas_call | solution.py:72
  13.0 12.4 %all-to-all-start = ((s32[64,1,128]{2,1,0:T(1,128)}), s32[64,1,128]{2,1,0:T(1,128)S(1)}, u32[]{:S(2)}, u32[]{:S(2)}) async-start(s32[64,1,128]{2,1,0:T(1,128)} %bitcast.40), calls=%async_computation | async-start | bytes 65536 | tf_op jit(solution)/shard_map/all_to_all | solution.py:468
  26.3 8.3 %all-to-all-done = s32[64,1,128]{2,1,0:T(1,128)S(1)} async-done(((s32[64,1,128]{2,1,0:T(1,128)}), s32[64,1,128]{2,1,0:T(1,128)S(1)}, u32[]{:S(2)}, u32[]{:S(2)}) %all-to-all-start) | async-done | bytes 32800 | tf_op jit(solution)/shard_map/all_to_all | solution.py:468
  35.2 7.3 %shard_map.115 = bf16[3072,128]{1,0:T(8,128)(2,1)} custom-call(s32[64,128]{1,0:T(8,128)} %bitcast.29, bf16[2048,128]{1,0:T(8,128)(2,1)} %convert_element_type.22.tb_ref), custom_call_target="tpu_custom_call" | custom-call | flops 1048576 | bytes 1024 | tf_op jit(solution)/shard_map/pallas_call | solution.py:162
  42.5 4.7 %all-to-all-start.2 = ((bf16[64,48,128]{2,1,0:T(8,128)(2,1)}), bf16[64,48,128]{2,1,0:T(8,128)(2,1)S(1)}, u32[]{:S(2)}, u32[]{:S(2)}) async-start(bf16[64,48,128]{2,1,0:T(8,128)(2,1)} %bitcast.28), calls=%async_computation.2 | async-start | bytes 1572864 | tf_op jit(solution)/shard_map/all_to_all | solution.py:443
  47.3 8.0 %shard_map.114 = bf16[3584,128]{1,0:T(8,128)(2,1)} custom-call(s32[64,128]{1,0:T(8,128)} %bitcast.30, bf16[2048,128]{1,0:T(8,128)(2,1)} %convert_element_type.22.tb_ref), custom_call_target="tpu_custom_call" | custom-call | flops 1048576 | bytes 1024 | tf_op jit(solution)/shard_map/pallas_call | solution.py:162
  55.2 15.1 %all-to-all-done.2 = bf16[64,48,128]{2,1,0:T(8,128)(2,1)S(1)} async-done(((bf16[64,48,128]{2,1,0:T(8,128)(2,1)}), bf16[64,48,128]{2,1,0:T(8,128)(2,1)S(1)}, u32[]{:S(2)}, u32[]{:S(2)}) %all-to-all-start.2) | async-done | bytes 786464 | tf_op jit(solution)/shard_map/all_to_all | solution.py:443
  70.4 6.5 %all-to-all-start.1 = ((bf16[64,56,128]{2,1,0:T(8,128)(2,1)}), bf16[64,56,128]{2,1,0:T(8,128)(2,1)S(1)}, u32[]{:S(2)}, u32[]{:S(2)}) async-start(bf16[64,56,128]{2,1,0:T(8,128)(2,1)} %bitcast.24), calls=%async_computation.1 | async-start | bytes 1835008 | tf_op jit(solution)/shard_map/all_to_all | solution.py:443
  78.1 3.0 %collective-permute-start.3 = (bf16[848,512]{1,0:T(8,128)(2,1)S(1)}, bf16[848,512]{1,0:T(8,128)(2,1)}, u32[]{:S(2)}, u32[]{:S(2)}) collective-permute-start(bf16[848,512]{1,0:T(8,128)(2,1)S(1)} %slice.14), channel_id=1, source_target_pairs={{0,3},{1,0},{2,1},{3,2},{4,7},{5,4},{6,5},{7,6},{8,11},{9,8},{10,9... | collective-permute-start | bytes 2605064 | tf_op jit(solution)/shard_map/ppermute | solution.py:450
  83.7 15.7 %collective-permute-done.3.refs_4_ = bf16[848,512]{1,0:T(8,128)(2,1)} collective-permute-done((bf16[848,512]{1,0:T(8,128)(2,1)S(1)}, bf16[848,512]{1,0:T(8,128)(2,1)}, u32[]{:S(2)}, u32[]{:S(2)}) %collective-permute-start.3) | collective-permute-done | bytes 868384 | tf_op jit(solution)/shard_map/ppermute | solution.py:450
  99.3 1.3 collective-permute-start.8
  100.6 4.9 %collective-permute-done.2.refs_3_ = bf16[832,512]{1,0:T(8,128)(2,1)} collective-permute-done((bf16[832,512]{1,0:T(8,128)(2,1)S(1)}, bf16[832,512]{1,0:T(8,128)(2,1)}, u32[]{:S(2)}, u32[]{:S(2)}) %collective-permute-start.2) | collective-permute-done | bytes 852000 | tf_op jit(solution)/shard_map/ppermute | solution.py:450
  106.9 3.4 %shard_map.113 = (f32[64,3328]{1,0:T(8,128)}, f32[64,3328]{1,0:T(8,128)}) custom-call(s32[13,4,256]{2,1,0:T(4,128)} %bitcast.33, s32[13,4,256]{2,1,0:T(4,128)} %bitcast.38, f32[13,4,256]{2,1,0:T(4,128)} %bitcast.35, f32[16,128]{1,0:T(8,128)} %get-tuple-element.19.rank_ref), custom_call_target="tpu_custom_call" | custom-call | flops 1048576 | bytes 1024 | tf_op jit(solution)/shard_map/pallas_call | solution.py:107
  110.3 8.7 %shard_map.116.refs_0_ = f32[128,3328]{1,0:T(8,128)} custom-call(f32[64,3328]{1,0:T(8,128)} %get-tuple-element.20.u_ref, f32[64,3328]{1,0:T(8,128)} %get-tuple-element.21.c_ref, bf16[3072,128]{1,0:T(8,128)(2,1)} %bitcast.21), custom_call_target="tpu_custom_call" | custom-call | flops 1048576 | bytes 1024 | tf_op jit(solution)/shard_map/pallas_call | solution.py:222
  120.0 9.8 %shard_map.117.x_ref = bf16[256,1664]{1,0:T(8,128)(2,1)} custom-call(f32[64,3328]{1,0:T(8,128)} %get-tuple-element.20.u_ref, f32[64,3328]{1,0:T(8,128)} %get-tuple-element.21.c_ref, bf16[3584,128]{1,0:T(8,128)(2,1)} %bitcast.19, f32[128,3328]{1,0:T(8,128)} %shard_map.116.refs_0_), custom_call_target="tpu_custom_call" | custom-call | flops 1048576 | bytes 1024 | tf_op jit(solution)/shard_map/pallas_call | solution.py:222
  130.7 14.4 %shard_map.119 = (bf16[1664,256]{1,0:T(8,128)(2,1)}, bf16[3328,128]{1,0:T(8,128)(2,1)}) custom-call(bf16[256,1664]{1,0:T(8,128)(2,1)} %shard_map.117.x_ref, f32[1,256]{1,0:T(1,128)} %bitcast.41, bf16[1680,512]{1,0:T(8,128)(2,1)} %shard_map.118.refs_0_, bf16[1680,512]{1,0:T(8,128)(2,1)} %collective-permute-done.refs_1_, ...), custom_call_target="tpu_custom_call" | custom-call | flops 1048576 | bytes 1024 | tf_op jit(solution)/shard_map/pallas_call | solution.py:292
  145.1 9.1 %shard_map.121 = bf16[3072,128]{1,0:T(8,128)(2,1)} custom-call(f32[64,3328]{1,0:T(8,128)} %get-tuple-element.20.u_ref, f32[64,3328]{1,0:T(8,128)} %get-tuple-element.21.c_ref, bf16[3328,128]{1,0:T(8,128)(2,1)} %get-tuple-element.29.d_ref), custom_call_target="tpu_custom_call" | custom-call | flops 1048576 | bytes 1024 | tf_op jit(solution)/shard_map/pallas_call | solution.py:322
  154.3 10.0 %all-to-all-start.4 = ((bf16[64,48,128]{2,1,0:T(8,128)(2,1)}), bf16[64,48,128]{2,1,0:T(8,128)(2,1)S(1)}, u32[]{:S(2)}, u32[]{:S(2)}) async-start(bf16[64,48,128]{2,1,0:T(8,128)(2,1)} %bitcast.27), calls=%async_computation.4 | async-start | bytes 1572864 | tf_op jit(solution)/shard_map/all_to_all | solution.py:443
  164.3 9.7 %shard_map.120 = bf16[3584,128]{1,0:T(8,128)(2,1)} custom-call(f32[64,3328]{1,0:T(8,128)} %get-tuple-element.20.u_ref, f32[64,3328]{1,0:T(8,128)} %get-tuple-element.21.c_ref, bf16[3328,128]{1,0:T(8,128)(2,1)} %get-tuple-element.29.d_ref), custom_call_target="tpu_custom_call" | custom-call | flops 1048576 | bytes 1024 | tf_op jit(solution)/shard_map/pallas_call | solution.py:322
  173.9 13.3 %all-to-all-done.4 = bf16[64,48,128]{2,1,0:T(8,128)(2,1)S(1)} async-done(((bf16[64,48,128]{2,1,0:T(8,128)(2,1)}), bf16[64,48,128]{2,1,0:T(8,128)(2,1)S(1)}, u32[]{:S(2)}, u32[]{:S(2)}) %all-to-all-start.4) | async-done | bytes 786464 | tf_op jit(solution)/shard_map/all_to_all | solution.py:443
  187.3 6.2 %all-to-all-start.3 = ((bf16[64,56,128]{2,1,0:T(8,128)(2,1)}), bf16[64,56,128]{2,1,0:T(8,128)(2,1)S(1)}, u32[]{:S(2)}, u32[]{:S(2)}) async-start(bf16[64,56,128]{2,1,0:T(8,128)(2,1)} %bitcast.25), calls=%async_computation.3 | async-start | bytes 1835008 | tf_op jit(solution)/shard_map/all_to_all | solution.py:443
  195.0 16.2 %shard_map.122 = f32[13,4,256]{2,1,0:T(4,128)} custom-call(s32[13,4,256]{2,1,0:T(4,128)} %bitcast.34, f32[13,4,256]{2,1,0:T(4,128)} %bitcast.36, f32[64,3328]{1,0:T(8,128)} %get-tuple-element.20.u_ref, bf16[1664,256]{1,0:T(8,128)(2,1)} %get-tuple-element.31.dt_ref, bf16[3072,128]{1,0:T(8,128)(2,1)} %bitcast.22, bf16[3584,128]{1,0:T(8,128)(2,1)} %bitcast.20), custom_call_target="tpu_custom_call" | custom-call | flops 1048576 | bytes 1024 | tf_op jit(solution)/shard_map/pallas_call | solution.py:382
  211.2 6.6 %shard_map.123.refs_0_ = f32[2048,128]{1,0:T(8,128)} custom-call(s32[1,3072]{1,0:T(1,128)} %reshape.46.list_ref, bf16[3072,128]{1,0:T(8,128)(2,1)} %bitcast.26), custom_call_target="tpu_custom_call" | custom-call | flops 1048576 | bytes 1024 | tf_op jit(solution)/shard_map/pallas_call | solution.py:425
  217.8 1.4 all-to-all-done.3
  220.1 7.8 %shard_map.124 = bf16[2048,128]{1,0:T(8,128)(2,1)} custom-call(s32[1,3584]{1,0:T(1,128)} %reshape.39.list_ref, bf16[3584,128]{1,0:T(8,128)(2,1)} %bitcast.23, f32[2048,128]{1,0:T(8,128)} %shard_map.123.refs_0_), custom_call_target="tpu_custom_call" | custom-call | flops 1048576 | bytes 1024 | tf_op jit(solution)/shard_map/pallas_call | solution.py:425
  230.8 4.7 %collective-permute-done.10 = bf16[512,128]{1,0:T(8,128)(2,1)S(1)} collective-permute-done((bf16[512,128]{1,0:T(8,128)(2,1)S(1)}, bf16[512,128]{1,0:T(8,128)(2,1)S(1)}, u32[]{:S(2)}, u32[]{:S(2)}) %collective-permute-start.10) | collective-permute-done | bytes 131104 | tf_op jit(solution)/shard_map/ppermute | solution.py:450
  235.5 3.5 %collective-permute-done.9 = bf16[512,128]{1,0:T(8,128)(2,1)S(1)} collective-permute-done((bf16[512,128]{1,0:T(8,128)(2,1)S(1)}, bf16[512,128]{1,0:T(8,128)(2,1)S(1)}, u32[]{:S(2)}, u32[]{:S(2)}) %collective-permute-start.9) | collective-permute-done | bytes 131104 | tf_op jit(solution)/shard_map/ppermute | solution.py:450
  240.9 1.9 collective-permute-start.14
  242.8 6.2 %collective-permute-done.12 = bf16[512,128]{1,0:T(8,128)(2,1)S(1)} collective-permute-done((bf16[512,128]{1,0:T(8,128)(2,1)S(1)}, bf16[512,128]{1,0:T(8,128)(2,1)S(1)}, u32[]{:S(2)}, u32[]{:S(2)}) %collective-permute-start.12) | collective-permute-done | bytes 131104 | tf_op jit(solution)/shard_map/ppermute | solution.py:450
  250.1 1.3 fusion.1
  (63 shorter events, 19.3 us)
Async XLA Ops:
  3.2 22.2 %copy-start.3 = (f32[2048,128]{1,0:T(8,128)S(1)}, f32[2048,128]{1,0:T(8,128)}, u32[]{:S(2)}) copy-start(f32[2048,128]{1,0:T(8,128)} %param.13) | copy-start | bytes 3145732
  6.1 70.7 %collective-permute-start.1 = (bf16[1680,512]{1,0:T(8,128)(2,1)}, bf16[1680,512]{1,0:T(8,128)(2,1)}, u32[]{:S(2)}, u32[]{:S(2)}) collective-permute-start(bf16[1680,512]{1,0:T(8,128)(2,1)} %shard_map.118.refs_0_), channel_id=1, source_target_pairs={{0,3},{1,0},{2,1},{3,2},{4,7},{5,4},{6,5},{7,6},{8,11},{9,8},{10,9... | collective-permute-start | bytes 5160968 | tf_op jit(solution)/shard_map/ppermute | solution.py:450
  9.7 72.2 %collective-permute-start = (bf16[1680,512]{1,0:T(8,128)(2,1)}, bf16[1680,512]{1,0:T(8,128)(2,1)}, u32[]{:S(2)}, u32[]{:S(2)}) collective-permute-start(bf16[1680,512]{1,0:T(8,128)(2,1)} %shard_map.118.refs_0_), channel_id=1, source_target_pairs={{0,1},{1,2},{2,3},{3,0},{4,5},{5,6},{6,7},{7,4},{8,9},{9,10},{10,1... | collective-permute-start | bytes 5160968 | tf_op jit(solution)/shard_map/ppermute | solution.py:450
  13.0 21.7 %all-to-all-start = ((s32[64,1,128]{2,1,0:T(1,128)}), s32[64,1,128]{2,1,0:T(1,128)S(1)}, u32[]{:S(2)}, u32[]{:S(2)}) async-start(s32[64,1,128]{2,1,0:T(1,128)} %bitcast.40), calls=%async_computation | async-start | bytes 65536 | tf_op jit(solution)/shard_map/all_to_all | solution.py:468
  34.6 0.6 copy-start.8
  42.5 27.9 %all-to-all-start.2 = ((bf16[64,48,128]{2,1,0:T(8,128)(2,1)}), bf16[64,48,128]{2,1,0:T(8,128)(2,1)S(1)}, u32[]{:S(2)}, u32[]{:S(2)}) async-start(bf16[64,48,128]{2,1,0:T(8,128)(2,1)} %bitcast.28), calls=%async_computation.2 | async-start | bytes 1572864 | tf_op jit(solution)/shard_map/all_to_all | solution.py:443
  70.4 7.7 %copy-start.1 = (bf16[64,48,128]{2,1,0:T(8,128)(2,1)}, bf16[64,48,128]{2,1,0:T(8,128)(2,1)S(1)}, u32[]{:S(2)}) copy-start(bf16[64,48,128]{2,1,0:T(8,128)(2,1)S(1)} %all-to-all-done.2) | copy-start | bytes 2359300
  70.4 10.7 %copy-start.2 = (bf16[1680,512]{1,0:T(8,128)(2,1)S(1)}, bf16[1680,512]{1,0:T(8,128)(2,1)}, u32[]{:S(2)}) copy-start(bf16[1680,512]{1,0:T(8,128)(2,1)} %shard_map.118.refs_0_) | copy-start | bytes 5160964
  70.4 48.7 %all-to-all-start.1 = ((bf16[64,56,128]{2,1,0:T(8,128)(2,1)}), bf16[64,56,128]{2,1,0:T(8,128)(2,1)S(1)}, u32[]{:S(2)}, u32[]{:S(2)}) async-start(bf16[64,56,128]{2,1,0:T(8,128)(2,1)} %bitcast.24), calls=%async_computation.1 | async-start | bytes 1835008 | tf_op jit(solution)/shard_map/all_to_all | solution.py:443
  76.8 29.5 %copy-start.11 = (bf16[256]{0:T(256)(128)(2,1)S(1)}, bf16[256]{0:T(256)(128)(2,1)}, u32[]{:S(2)}) copy-start(bf16[256]{0:T(256)(128)(2,1)} %param.12) | copy-start | bytes 1540
  78.1 21.2 %collective-permute-start.3 = (bf16[848,512]{1,0:T(8,128)(2,1)S(1)}, bf16[848,512]{1,0:T(8,128)(2,1)}, u32[]{:S(2)}, u32[]{:S(2)}) collective-permute-start(bf16[848,512]{1,0:T(8,128)(2,1)S(1)} %slice.14), channel_id=1, source_target_pairs={{0,3},{1,0},{2,1},{3,2},{4,7},{5,4},{6,5},{7,6},{8,11},{9,8},{10,9... | collective-permute-start | bytes 2605064 | tf_op jit(solution)/shard_map/ppermute | solution.py:450
  81.1 48.7 %collective-permute-start.4 = (bf16[1680,512]{1,0:T(8,128)(2,1)S(1)}, bf16[1680,512]{1,0:T(8,128)(2,1)}, u32[]{:S(2)}, u32[]{:S(2)}) collective-permute-start(bf16[1680,512]{1,0:T(8,128)(2,1)S(1)} %copy-done.2), channel_id=1, source_target_pairs={{0,4},{4,0},{8,12},{12,8},{16,20},{20,16},{24,28},{28,24},{32,36},... | collective-permute-start | bytes 5160968 | tf_op jit(solution)/shard_map/ppermute | solution.py:454
  81.8 47.9 %collective-permute-start.5 = (bf16[1680,512]{1,0:T(8,128)(2,1)}, bf16[1680,512]{1,0:T(8,128)(2,1)}, u32[]{:S(2)}, u32[]{:S(2)}) collective-permute-start(bf16[1680,512]{1,0:T(8,128)(2,1)} %collective-permute-done.refs_1_), channel_id=1, source_target_pairs={{0,4},{4,0},{8,12},{12,8},{16,20},{20,16},{24,28},{28,24},{32,36},... | collective-permute-start | bytes 5160968 | tf_op jit(solution)/shard_map/ppermute | solution.py:454
  81.9 47.9 %collective-permute-start.6 = (bf16[1680,512]{1,0:T(8,128)(2,1)}, bf16[1680,512]{1,0:T(8,128)(2,1)}, u32[]{:S(2)}, u32[]{:S(2)}) collective-permute-start(bf16[1680,512]{1,0:T(8,128)(2,1)} %collective-permute-done.1.refs_2_), channel_id=1, source_target_pairs={{0,4},{4,0},{8,12},{12,8},{16,20},{20,16},{24,28},{28,24},{32,36},... | collective-permute-start | bytes 5160968 | tf_op jit(solution)/shard_map/ppermute | solution.py:454
  83.6 21.9 %collective-permute-start.2 = (bf16[832,512]{1,0:T(8,128)(2,1)S(1)}, bf16[832,512]{1,0:T(8,128)(2,1)}, u32[]{:S(2)}, u32[]{:S(2)}) collective-permute-start(bf16[832,512]{1,0:T(8,128)(2,1)S(1)} %slice.13), channel_id=1, source_target_pairs={{0,1},{1,2},{2,3},{3,0},{4,5},{5,6},{6,7},{7,4},{8,9},{9,10},{10,1... | collective-permute-start | bytes 2555912 | tf_op jit(solution)/shard_map/ppermute | solution.py:450
  99.3 30.5 %collective-permute-start.8 = (bf16[848,512]{1,0:T(8,128)(2,1)}, bf16[848,512]{1,0:T(8,128)(2,1)S(1)}, u32[]{:S(2)}, u32[]{:S(2)}) collective-permute-start(bf16[848,512]{1,0:T(8,128)(2,1)} %collective-permute-done.3.refs_4_), channel_id=1, source_target_pairs={{0,4},{4,0},{8,12},{12,8},{16,20},{20,16},{24,28},{28,24},{32,36},... | collective-permute-start | bytes 2605064 | tf_op jit(solution)/shard_map/ppermute | solution.py:454
  105.5 24.3 %collective-permute-start.7 = (bf16[832,512]{1,0:T(8,128)(2,1)}, bf16[832,512]{1,0:T(8,128)(2,1)}, u32[]{:S(2)}, u32[]{:S(2)}) collective-permute-start(bf16[832,512]{1,0:T(8,128)(2,1)} %collective-permute-done.2.refs_3_), channel_id=1, source_target_pairs={{0,4},{4,0},{8,12},{12,8},{16,20},{20,16},{24,28},{28,24},{32,36},... | collective-permute-start | bytes 2555912 | tf_op jit(solution)/shard_map/ppermute | solution.py:454
  119.1 0.9 copy-start
  129.8 0.9 copy-start.7
  154.3 33.0 %all-to-all-start.4 = ((bf16[64,48,128]{2,1,0:T(8,128)(2,1)}), bf16[64,48,128]{2,1,0:T(8,128)(2,1)S(1)}, u32[]{:S(2)}, u32[]{:S(2)}) async-start(bf16[64,48,128]{2,1,0:T(8,128)(2,1)} %bitcast.27), calls=%async_computation.4 | async-start | bytes 1572864 | tf_op jit(solution)/shard_map/all_to_all | solution.py:443
  173.9 19.6 %copy-start.9 = (s32[64,1,128]{2,1,0:T(1,128)S(1)}, s32[64,1,128]{2,1,0:T(1,128)}, u32[]{:S(2)}) copy-start(s32[64,1,128]{2,1,0:T(1,128)} %copy-done.8) | copy-start | bytes 98308
  187.3 23.9 %copy-start.6 = (bf16[64,48,128]{2,1,0:T(8,128)(2,1)}, bf16[64,48,128]{2,1,0:T(8,128)(2,1)S(1)}, u32[]{:S(2)}) copy-start(bf16[64,48,128]{2,1,0:T(8,128)(2,1)S(1)} %all-to-all-done.4) | copy-start | bytes 2359300
  187.3 31.9 %all-to-all-start.3 = ((bf16[64,56,128]{2,1,0:T(8,128)(2,1)}), bf16[64,56,128]{2,1,0:T(8,128)(2,1)S(1)}, u32[]{:S(2)}, u32[]{:S(2)}) async-start(bf16[64,56,128]{2,1,0:T(8,128)(2,1)} %bitcast.25), calls=%async_computation.3 | async-start | bytes 1835008 | tf_op jit(solution)/shard_map/all_to_all | solution.py:443
  219.2 0.9 copy-start.5
  228.0 21.5 %copy-start.10 = (f32[2048]{0:T(1024)S(1)}, f32[2048]{0:T(1024)}, u32[]{:S(2)}) copy-start(f32[2048]{0:T(1024)} %param.14) | copy-start | bytes 24580
  228.0 22.1 %copy-start.4 = (f32[2048,128]{1,0:T(8,128)S(1)}, f32[2048,128]{1,0:T(8,128)}, u32[]{:S(2)}) copy-start(f32[2048,128]{1,0:T(8,128)} %param.13) | copy-start | bytes 3145732
  229.1 6.4 %collective-permute-start.10 = (bf16[512,128]{1,0:T(8,128)(2,1)S(1)}, bf16[512,128]{1,0:T(8,128)(2,1)S(1)}, u32[]{:S(2)}, u32[]{:S(2)}) collective-permute-start(bf16[512,128]{1,0:T(8,128)(2,1)S(1)} %get-tuple-element.39), channel_id=1, source_target_pairs={{0,2},{1,3},{2,0},{3,1},{4,6},{5,7},{6,4},{7,5},{8,10},{9,11},{10,... | collective-permute-start | bytes 393224 | tf_op jit(solution)/shard_map/ppermute | solution.py:450
  229.2 6.3 %collective-permute-start.11 = (bf16[512,128]{1,0:T(8,128)(2,1)S(1)}, bf16[512,128]{1,0:T(8,128)(2,1)S(1)}, u32[]{:S(2)}, u32[]{:S(2)}) collective-permute-start(bf16[512,128]{1,0:T(8,128)(2,1)S(1)} %get-tuple-element.38), channel_id=1, source_target_pairs={{0,3},{1,0},{2,1},{3,2},{4,7},{5,4},{6,5},{7,6},{8,11},{9,8},{10,9... | collective-permute-start | bytes 393224 | tf_op jit(solution)/shard_map/ppermute | solution.py:450
  230.4 8.5 %collective-permute-start.9 = (bf16[512,128]{1,0:T(8,128)(2,1)S(1)}, bf16[512,128]{1,0:T(8,128)(2,1)S(1)}, u32[]{:S(2)}, u32[]{:S(2)}) collective-permute-start(bf16[512,128]{1,0:T(8,128)(2,1)S(1)} %get-tuple-element.37), channel_id=1, source_target_pairs={{0,1},{1,2},{2,3},{3,0},{4,5},{5,6},{6,7},{7,4},{8,9},{9,10},{10,1... | collective-permute-start | bytes 393224 | tf_op jit(solution)/shard_map/ppermute | solution.py:450
  240.0 9.0 %collective-permute-start.12 = (bf16[512,128]{1,0:T(8,128)(2,1)S(1)}, bf16[512,128]{1,0:T(8,128)(2,1)S(1)}, u32[]{:S(2)}, u32[]{:S(2)}) collective-permute-start(bf16[512,128]{1,0:T(8,128)(2,1)S(1)} %get-tuple-element.36), channel_id=1, source_target_pairs={{0,1},{1,2},{2,3},{3,0},{4,5},{5,6},{6,7},{7,4},{8,9},{9,10},{10,1... | collective-permute-start | bytes 393224 | tf_op jit(solution)/shard_map/ppermute | solution.py:450
  240.1 8.9 %collective-permute-start.13 = (bf16[512,128]{1,0:T(8,128)(2,1)S(1)}, bf16[512,128]{1,0:T(8,128)(2,1)S(1)}, u32[]{:S(2)}, u32[]{:S(2)}) collective-permute-start(bf16[512,128]{1,0:T(8,128)(2,1)S(1)} %get-tuple-element.36), channel_id=1, source_target_pairs={{0,2},{1,3},{2,0},{3,1},{4,6},{5,7},{6,4},{7,5},{8,10},{9,11},{10,... | collective-permute-start | bytes 393224 | tf_op jit(solution)/shard_map/ppermute | solution.py:450
  240.9 8.1 %collective-permute-start.14 = (bf16[512,128]{1,0:T(8,128)(2,1)S(1)}, bf16[512,128]{1,0:T(8,128)(2,1)S(1)}, u32[]{:S(2)}, u32[]{:S(2)}) collective-permute-start(bf16[512,128]{1,0:T(8,128)(2,1)S(1)} %get-tuple-element.36), channel_id=1, source_target_pairs={{0,3},{1,0},{2,1},{3,2},{4,7},{5,4},{6,5},{7,6},{8,11},{9,8},{10,9... | collective-permute-start | bytes 393224 | tf_op jit(solution)/shard_map/ppermute | solution.py:450
